TPU v7x, 32 devices: a whole 2x2x4 slice. The times are simulated.
32 devices in a mesh: ex: 8 (over z, core), pd: 4 (over y, x).
Axes of the slice: x: 2, y: 2, z: 4, core: 2. Of those that a mesh axis runs over, the one named last changes fastest.
Arguments:
- verdict_states: bfloat16 [2048, 8192], P(('ex', 'pd')), may hold values from -6 to 6
- verdict_labels: int32 [64], replicated, may hold values from 0 to 1
- partner: int32 [64], replicated, may hold values from 0 to 63, as said below
- gate_weight: bfloat16 [8192, 28672], P(None, ('ex', 'pd')), may hold values from -0.0625 to 0.0625
- up_weight: bfloat16 [8192, 28672], P(None, ('ex', 'pd')), may hold values from -0.0625 to 0.0625
- down_weight: bfloat16 [28672, 8192], P(('ex', 'pd')), may hold values from -0.03125 to 0.03125
- readout: bfloat16 [8192], replicated, may hold values from -0.8984375 to 0.8984375
- sketch_in: bfloat16 [64, 8192], replicated, may hold values from -0.0625 to 0.0625
- sketch_out: bfloat16 [64, 28672], P(None, ('ex', 'pd')), may hold values from -6 to 6
- store: bfloat16 [65536, 4096], P('ex', 'pd'), may hold values from -0.099609375 to 0.099609375
- source_ids: int32 [65536], P('ex'), may hold values from 0 to 511
Outputs:
- contrast: float32 [64, 65536], P('pd', 'ex')
- source_scores: float32 [64, 512], P('pd')
Inputs may be any that keep to these rules, and one draw needn't show every extreme that they name: partner[partner[r]] = r and partner[r] != r for every row r.
All inputs are finite; a program needn't handle non-finite values.
Results may differ from a plain program's by a relative error of at most 0.013.
Values may be sent and summed in bfloat16 or wider, within the bound.
No kernel may reach another device: no remote copies, remote signals or barrier semaphores. Data moves between devices by JAX's collectives and lax.ppermute only.
A program may use at most 192 MiB of HBM per device.

v0:
```python
import functools

import jax
import jax.numpy as jnp
from jax import lax
from jax.experimental import pallas as pl
from jax.experimental.pallas import tpu as pltpu
from jax.sharding import Mesh
from jax.sharding import PartitionSpec as P

SOURCES = 512
CORES = 2
SPLIT = 4
CONTRACT = (((1,), (1,)), ((), ()))


def swap(value, axis, mask):
    size = lax.axis_size(axis)
    return lax.ppermute(value, axis, [(i, i ^ mask) for i in range(size)])


def turn(value, axis, shift):
    size = lax.axis_size(axis)
    return lax.ppermute(value, axis, [(i, (i + shift) % size) for i in range(size)])


def pick(value, index, axis):
    return lax.dynamic_index_in_dim(value, index, axis, keepdims=False)


def reduce_rows(part):
    rows, parts, width = part.shape
    core, pd = lax.axis_index("core"), lax.axis_index("pd")
    halves = part.reshape(CORES, rows // CORES, parts, width)
    half = pick(halves, core, 0) + swap(pick(halves, 1 - core, 0), "core", 1)
    total = pick(half, pd, 1)
    for k in range(1, parts):
        total = total + swap(pick(half, pd ^ k, 1), "pd", k)
    whole = total
    for k in range(1, lax.axis_size("chip")):
        whole = whole + turn(total, "chip", k)
    other = swap(whole, "core", 1)
    first = jnp.where(core == 0, whole, other)
    second = jnp.where(core == 0, other, whole)
    return jnp.concatenate([first, second], axis=0)


def layer_kernel(count, length, *refs):
    pieces = refs[:count]
    gate_w, up_w, sin, sout, wvec, proj, lrow, x, w, acc, dgate, sems = refs[count:]
    step = pl.program_id(0)
    steps = pl.num_programs(0)
    block = x.shape[1]
    features = gate_w.shape[1]
    tokens = pieces[0].shape[0]
    kin = sin.shape[0]

    def copies(k):
        slot = lax.rem(k, 2)
        here = pl.ds(pl.multiple_of(k * block, block), block)
        return [
            pltpu.make_async_copy(
                weight.at[here, :],
                w.at[slot, :, pl.ds(i * features, features)],
                sems.at[slot, i],
            )
            for i, weight in enumerate((gate_w, up_w))
        ]

    @pl.when(step == 0)
    def _():
        for copy in copies(step):
            copy.start()
        acc[...] = jnp.zeros_like(acc)
        proj[...] = jnp.zeros_like(proj)

    @pl.when(step + 1 < steps)
    def _():
        for copy in copies(step + 1):
            copy.start()

    for i, piece in enumerate(pieces):
        x[i * tokens : (i + 1) * tokens, :] = piece[...]
    for copy in copies(step):
        copy.wait()
    proj[:, :kin] += lax.dot_general(x[...], sin[...], CONTRACT, preferred_element_type=jnp.float32)
    acc[...] += jnp.dot(x[...], w[lax.rem(step, 2)], preferred_element_type=jnp.float32)

    @pl.when(step == steps - 1)
    def _():
        @pl.loop(0, acc.shape[0] // length)
        def _(i):
            here = pl.ds(pl.multiple_of(i * length, length), length)
            total = jnp.zeros((length, 128), jnp.float32)
            for j in range(features // 128):
                at = slice(j * 128, (j + 1) * 128)
                gate = acc[here, at]
                weighted = acc[here, features + j * 128 : features + (j + 1) * 128] * wvec[:, at]
                sig = jax.nn.sigmoid(gate)
                swish = gate * sig
                total = total + swish * weighted
                dgate[here, at] = (weighted * (sig + swish * (1.0 - sig))).astype(jnp.bfloat16)
            lrow[pl.ds(pl.multiple_of(8 * i, 8), 8), :] = total.reshape(-1, 8, 128).sum(axis=0)

        proj[:, kin:] = lax.dot_general(
            dgate[...], sout[...], CONTRACT, preferred_element_type=jnp.float32
        )


def layer(pieces, gate_weight, up_weight, sketch_in, sketch_out, wvec, length):
    count = len(pieces)
    tokens, depth = pieces[0].shape
    total = count * tokens
    features = gate_weight.shape[1]
    kin, kout = sketch_in.shape[0], sketch_out.shape[0]
    rows = total // length
    block = min(1024, depth)
    return pl.pallas_call(
        functools.partial(layer_kernel, count, length),
        grid=(depth // block,),
        in_specs=[pl.BlockSpec((tokens, block), lambda k: (0, k))] * count
        + [
            pl.BlockSpec(memory_space=pl.ANY),
            pl.BlockSpec(memory_space=pl.ANY),
            pl.BlockSpec((kin, block), lambda k: (0, k)),
            pl.BlockSpec((kout, features), lambda k: (0, 0)),
            pl.BlockSpec((1, features), lambda k: (0, 0)),
        ],
        out_specs=[
            pl.BlockSpec((total, kin + kout), lambda k: (0, 0)),
            pl.BlockSpec((rows * 8, 128), lambda k: (0, 0)),
        ],
        out_shape=[
            jax.ShapeDtypeStruct((total, kin + kout), jnp.float32),
            jax.ShapeDtypeStruct((rows * 8, 128), jnp.float32),
        ],
        scratch_shapes=[
            pltpu.VMEM((total, block), jnp.bfloat16),
            pltpu.VMEM((2, block, 2 * features), jnp.bfloat16),
            pltpu.VMEM((total, 2 * features), jnp.float32),
            pltpu.VMEM((total, features), jnp.bfloat16),
            pltpu.SemaphoreType.DMA((2, 2)),
        ],
        compiler_params=pltpu.CompilerParams(vmem_limit_bytes=60 * 1024 * 1024),
        cost_estimate=pl.CostEstimate(
            flops=4 * total * depth * features,
            bytes_accessed=2 * depth * (2 * features + total),
            transcendentals=total * features,
        ),
    )(*pieces, gate_weight, up_weight, sketch_in, sketch_out, wvec)


def prepare_kernel(ids, readout, *refs):
    stores, downs = refs[:SPLIT], refs[SPLIT : 2 * SPLIT]
    table, wvec, acc = refs[2 * SPLIT :]
    step = pl.program_id(0)

    @pl.when(step == 0)
    def _():
        acc[...] = jnp.zeros_like(acc)
        wvec[...] = jnp.zeros_like(wvec)

    sources = acc.shape[0]
    part = stores[0].shape[0]
    labels = lax.broadcasted_iota(jnp.int32, (sources, part), 0)
    for i, store in enumerate(stores):
        onehot = jnp.where(labels == ids[:, i * part : (i + 1) * part], 1.0, 0.0)
        acc[...] += jnp.dot(
            onehot.astype(jnp.bfloat16), store[...], preferred_element_type=jnp.float32
        )
    for i, down in enumerate(downs):
        wvec[i] += lax.dot_general(
            readout[...], down[...], CONTRACT, preferred_element_type=jnp.float32
        )

    @pl.when(step == pl.num_programs(0) - 1)
    def _():
        high = acc[...].astype(jnp.bfloat16)
        table[:sources, :] = high
        table[sources:, :] = (acc[...] - high.astype(jnp.float32)).astype(jnp.bfloat16)


def prepare(store, source_ids, down_weight, readout):
    examples, width = store.shape
    features, depth = down_weight.shape
    steps = 8
    block, deep = examples // steps, depth // steps
    part, piece = block // SPLIT, features // SPLIT
    table, wvec = pl.pallas_call(
        prepare_kernel,
        grid=(steps,),
        in_specs=[
            pl.BlockSpec((1, block), lambda k: (0, k)),
            pl.BlockSpec((8, deep), lambda k: (0, k)),
        ]
        + [pl.BlockSpec((part, width), lambda k, i=i: (k * SPLIT + i, 0)) for i in range(SPLIT)]
        + [pl.BlockSpec((piece, deep), lambda k, i=i: (i, k)) for i in range(SPLIT)],
        out_specs=[
            pl.BlockSpec((2 * SOURCES, width), lambda k: (0, 0)),
            pl.BlockSpec((SPLIT, 8, piece), lambda k: (0, 0, 0)),
        ],
        out_shape=[
            jax.ShapeDtypeStruct((2 * SOURCES, width), jnp.bfloat16),
            jax.ShapeDtypeStruct((SPLIT, 8, piece), jnp.float32),
        ],
        scratch_shapes=[pltpu.VMEM((SOURCES, width), jnp.float32)],
        compiler_params=pltpu.CompilerParams(vmem_limit_bytes=60 * 1024 * 1024),
        cost_estimate=pl.CostEstimate(
            flops=2 * SOURCES * examples * width,
            bytes_accessed=2 * examples * width + 2 * features * depth,
            transcendentals=0,
        ),
    )(
        source_ids.reshape(1, -1),
        jnp.broadcast_to(readout[None, :], (8, depth)),
        *[store] * SPLIT,
        *[down_weight] * SPLIT,
    )
    return table, wvec[:, 0].reshape(1, features)


def add_logit(sketch, logit, parts):
    rows = sketch.shape[0]
    wide = jnp.broadcast_to(logit[:, None, None], (rows, parts, 128))
    return jnp.concatenate([sketch.reshape(rows, parts, -1), wide], axis=2)


def sibling(value):
    return swap(value, "core", 1)


def plane_perm(masks):
    parts = lax.axis_size("pd")
    return [
        (core * parts + pd, core * parts + (pd ^ masks[core]))
        for core in range(CORES)
        for pd in range(parts)
    ]


def pack(sketch, logit):
    high = logit.astype(jnp.bfloat16)
    low = (logit - high.astype(jnp.float32)).astype(jnp.bfloat16)
    return jnp.concatenate([sketch.astype(jnp.bfloat16), high, low], axis=-1)


def add_packed(sketch, logit, packed):
    width, lanes = sketch.shape[-1], logit.shape[-1]
    high, low = packed[..., width : width + lanes], packed[..., width + lanes :]
    return (
        sketch + packed[..., :width].astype(jnp.float32),
        logit + (high.astype(jnp.float32) + low.astype(jnp.float32)),
    )


def ring_order(row, rows):
    chips = lax.axis_size("chip")
    place, core = lax.axis_index("chip"), lax.axis_index("core")
    per = rows // (CORES * chips)
    at_layer, at_core, at = row // (CORES * per), row // per % CORES, row % per
    return ((at_core != core) * chips + (place - at_layer) % chips) * per + at


def ring_rows(rows):
    chips = lax.axis_size("chip")
    place, core = lax.axis_index("chip"), lax.axis_index("core")
    per = rows // (CORES * chips)
    at = jnp.arange(rows)
    half, step = at // (chips * per), at // per % chips
    return ((place - step) % chips * CORES + (core ^ half)) * per + at % per


def piped_sketches(
    states, gate_weight, up_weight, wvec, table, sketch_in, sketch_out, rows, length, extras
):
    parts, chips = lax.axis_size("pd"), lax.axis_size("chip")
    place, core, pd = lax.axis_index("chip"), lax.axis_index("core"), lax.axis_index("pd")
    mine = states.shape[0]
    kin, kout = sketch_in.shape[0], sketch_out.shape[0]
    first, second = (2, 1), (1, 2)
    plane = ("core", "pd")
    tie = lax.optimization_barrier

    def send_a(value):
        return lax.ppermute(value, plane, plane_perm(first))

    def send_b(value):
        return lax.ppermute(value, plane, plane_perm(second))

    def ring(value, shift=1):
        return turn(value, "chip", shift)

    sin = sketch_in.reshape(parts, kin // parts, -1)[jnp.arange(parts) ^ pd]
    sin = sin.reshape(sketch_in.shape)

    def run(*pieces):
        return layer(pieces, gate_weight, up_weight, sin, sketch_out, wvec, length)

    p0 = states
    p0s = sibling(p0)
    a0, b0, p1 = send_a(p0), send_b(p0), ring(p0)
    a0, b0, table, wvec, sin = tie((a0, b0, table, wvec, sin))
    a0, p0 = tie((a0, p0))
    p3 = ring(p0, -1)
    a0s, b0s = sibling(a0), sibling(b0)
    a1, b1 = send_a(p1), send_b(p1)
    d0 = send_b(a0)
    out0 = run(p0, p0s, a0, a0s, b0, b0s)
    extras = extras(out0[1])
    p1s = sibling(p1)
    p1, p3, out0 = tie((p1, p3, out0))
    a1, b1, d0, out0 = tie((a1, b1, d0, out0))
    a3, b3, p2 = send_a(p3), send_b(p3), ring(p1)
    a1s, b1s, d0s = sibling(a1), sibling(b1), sibling(d0)
    d1 = send_b(a1)
    d0s, extras = tie((d0s, extras))
    out1 = run(d0, d0s, p1, p1s, a1, a1s, b1, b1s)
    p3s = sibling(p3)
    a3, b3, d1, p2, out1 = tie((a3, b3, d1, p2, out1))
    a2, b2, d2 = send_a(p2), send_b(p2), ring(d1)
    d3 = send_b(a3)
    a3s, b3s, d1s = sibling(a3), sibling(b3), sibling(d1)
    out2 = run(d1, d1s, p3, p3s, a3, a3s, b3, b3s)
    p2s = sibling(p2)
    a2, b2, d2, d3, out2 = tie((a2, b2, d2, d3, out2))
    out3 = run(
        d3, sibling(d3), p2, p2s, a2, sibling(a2), b2, sibling(b2), d2, sibling(d2)
    )
    outs = (out0, out1, out2, out3)
    place_of = jnp.array([0, 1, 3, 2])

    cores = (core + jnp.arange(CORES)) % CORES
    apart = jnp.arange(parts)[None, :] ^ pd
    is_a = jnp.where(cores[:, None] == 0, apart == first[0], apart == first[1])
    slot = jnp.where(apart == 0, 0, jnp.where(apart == 3, 6, jnp.where(is_a, 2, 4)))
    slot = slot + jnp.arange(CORES)[:, None]
    order = slot[:, None, :] + 2 * parts * place_of[None, :, None]
    order = order.reshape(-1)
    pieces = order.shape[0]
    proj = jnp.concatenate([o[0] for o in outs]).reshape(pieces, -1, kin + kout)[order]
    logit = jnp.concatenate([o[1] for o in outs]).reshape(pieces, -1, 8 * 128).sum(axis=2)[order]
    proj = proj.reshape(rows, length, kin + kout)
    sketch = jnp.einsum(
        "rti,rto->rio", proj[:, :, :kin], proj[:, :, kin:], precision=lax.Precision.HIGH
    ).reshape(rows, kin * kout)
    wide = jnp.broadcast_to(logit.reshape(rows, 1), (rows, 128))
    part = jnp.concatenate([sketch, wide], axis=1)
    half = part[: rows // CORES] + sibling(part[rows // CORES :])
    width = kin * kout // parts
    blocks = [half[:, k * width : (k + 1) * width] for k in range(parts)]
    lanes = half[:, kin * kout : kin * kout + 64]
    sketch, logit = blocks[0], lanes
    for k in range(1, parts):
        sketch, logit = add_packed(sketch, logit, swap(pack(blocks[k], lanes), "pd", k))
    sketch, logit = (v.reshape(chips, -1, v.shape[1]) for v in (sketch, logit))
    packed = pack(sketch, logit)
    for k in range(1, chips):
        sketch, logit = add_packed(sketch, logit, jnp.roll(ring(packed, k), k, axis=0))
    whole = jnp.concatenate([sketch, logit, logit], axis=-1).reshape(rows // CORES, -1)
    both = jnp.concatenate([whole, sibling(whole)])
    return both, table, extras


def contrast_kernel(with_table, diff, *refs):
    step = pl.program_id(0)
    lead = 1 if with_table else 0
    table, stores, outs = refs[:lead], refs[lead : lead + SPLIT], refs[lead + SPLIT :]
    mine = outs[0].shape[0]

    if with_table:

        @pl.when(step == 0)
        def _():
            both = lax.dot_general(
                table[0][...], diff[...], CONTRACT, preferred_element_type=jnp.float32
            ).T
            half = both.shape[1] // 2
            score = both[:, :half] + both[:, half:]
            high = score.astype(jnp.bfloat16)
            low = (score - high.astype(jnp.float32)).astype(jnp.bfloat16)
            for i, out in enumerate(outs):
                out[:, :half] = high[i * mine : (i + 1) * mine]
                out[:, half:] = low[i * mine : (i + 1) * mine]

    @pl.when(step >= lead)
    def _():
        for j, store in enumerate(stores):
            part = lax.dot_general(
                store[...], diff[...], CONTRACT, preferred_element_type=jnp.float32
            ).T
            size = part.shape[1]
            for i, out in enumerate(outs):
                out[:, j * size : (j + 1) * size] = part[i * mine : (i + 1) * mine].astype(
                    out.dtype
                )


def contrast_parts(diff, store, first, blocks, parts, table=None):
    rows, width = diff.shape
    block = 2 * SOURCES
    lead = 0 if table is None else 1
    mine = rows // parts
    columns = block * (blocks + lead)
    tables = [] if table is None else [table]

    def stored(i):
        return pl.BlockSpec(
            (block // SPLIT, width),
            lambda k: ((first + jnp.maximum(k - lead, 0)) * SPLIT + i, 0),
        )

    return pl.pallas_call(
        functools.partial(contrast_kernel, table is not None),
        grid=(blocks + lead,),
        in_specs=[pl.BlockSpec((rows, width), lambda k: (0, 0))]
        + [pl.BlockSpec((block, width), lambda k: (0, 0))] * lead
        + [stored(i) for i in range(SPLIT)],
        out_specs=[pl.BlockSpec((mine, block), lambda k: (0, k))] * parts,
        out_shape=[jax.ShapeDtypeStruct((mine, columns), jnp.bfloat16)] * parts,
        compiler_params=pltpu.CompilerParams(vmem_limit_bytes=60 * 1024 * 1024),
        cost_estimate=pl.CostEstimate(
            flops=2 * rows * width * columns,
            bytes_accessed=2 * (width + rows) * columns,
            transcendentals=0,
        ),
    )(diff, *tables, *[store] * SPLIT)


def exchange(blocks):
    total = blocks[0].astype(jnp.float32)
    for k in range(1, len(blocks)):
        total = total + swap(blocks[k], "pd", k).astype(jnp.float32)
    return total


def plain_sketches(
    states, gate_weight, up_weight, wvec, table, sketch_in, sketch_out, rows, length, extras
):
    kin, kout = sketch_in.shape[0], sketch_out.shape[0]
    ff_local = gate_weight.shape[1]
    states = lax.all_gather(states, ("chip", "core", "pd"), axis=0, tiled=True)
    gate = jnp.dot(states, gate_weight, preferred_element_type=jnp.float32)
    up = jnp.dot(states, up_weight, preferred_element_type=jnp.float32)
    ain = lax.dot_general(states, sketch_in, CONTRACT, preferred_element_type=jnp.float32)
    sig = jax.nn.sigmoid(gate)
    weighted = up * wvec
    logit = jnp.sum((gate * sig * weighted).reshape(rows, length * ff_local), axis=1)
    dgate = (weighted * sig * (1.0 + gate * (1.0 - sig))).astype(jnp.bfloat16)
    bout = lax.dot_general(dgate, sketch_out, CONTRACT, preferred_element_type=jnp.float32)
    sketch = jnp.einsum(
        "rti,rto->rio",
        ain.reshape(rows, length, kin),
        bout.reshape(rows, length, kout),
        precision=lax.Precision.HIGHEST,
    ).reshape(rows, kin * kout)
    reduced = reduce_rows(add_logit(sketch, logit, lax.axis_size("pd")))
    return reduced, table, extras(reduced)


def on_device(
    verdict_states,
    verdict_labels,
    partner,
    gate_weight,
    up_weight,
    down_weight,
    readout,
    sketch_in,
    sketch_out,
    store,
    source_ids,
):
    rows = verdict_labels.shape[0]
    parts, chips = lax.axis_size("pd"), lax.axis_size("chip")
    pd = lax.axis_index("pd")
    examples, width = store.shape
    mine = verdict_states.shape[0]
    length = mine * parts * CORES * chips // rows

    table, wvec = prepare(store, source_ids, down_weight, readout)
    piped = (
        parts == 4
        and chips == 4
        and mine == 2 * length
        and length == 32
        and gate_weight.shape[1] % 128 == 0
        and gate_weight.shape[0] % 2048 == 0
        and gate_weight.shape[0] >= 6144
    )
    sketches = piped_sketches if piped else plain_sketches
    group = rows // parts

    def extras(after):
        mates, labels, _ = lax.optimization_barrier((partner, verdict_labels, after))
        order = jnp.concatenate([(pd ^ k) * group + jnp.arange(group) for k in range(parts)])
        own, mate = order, mates[order]
        if piped:
            labels = labels[ring_rows(rows)]
            own, mate = ring_order(own, rows), ring_order(mate, rows)
        return 2.0 * labels.astype(jnp.float32) - 1.0, own, mate

    reduced, table, extras = sketches(
        verdict_states,
        gate_weight,
        up_weight,
        wvec,
        table,
        sketch_in,
        sketch_out,
        rows,
        length,
        extras,
    )
    sign, mine_at, mate_at = extras

    coef = -sign * jax.nn.sigmoid(-sign * (reduced[:, width] / length))
    scaled = reduced[:, :width] * (coef / length)[:, None]
    diff = (scaled[mine_at] - scaled[mate_at]).astype(jnp.bfloat16)

    blocks = examples // (2 * SOURCES)
    early = blocks // 2
    front = exchange(contrast_parts(diff, store, 0, early, parts, table))
    back = exchange(contrast_parts(diff, store, early, blocks - early, parts))
    scores = front[:, :SOURCES] + front[:, SOURCES : 2 * SOURCES]
    whole = scores
    for k in range(1, chips):
        whole = whole + turn(scores, "chip", k)
    whole = whole + sibling(whole)
    factor = (SOURCES / (examples * CORES * chips)) ** 0.5
    contrast = jnp.concatenate([front[:, 2 * SOURCES :], back], axis=1)
    return (contrast, whole * factor)


def solution(mesh):
    ex, pd = mesh.shape["ex"], mesh.shape["pd"]
    axed = Mesh(mesh.devices.reshape(ex // CORES, CORES, pd), ("chip", "core", "pd"))
    every = ("chip", "core", "pd")
    in_specs = (
        P(every, None),
        P(),
        P(),
        P(None, every),
        P(None, every),
        P(every, None),
        P(),
        P(),
        P(None, every),
        P(("chip", "core"), "pd"),
        P(("chip", "core")),
    )
    out_specs = (P("pd", ("chip", "core")), P("pd", None))
    return jax.shard_map(
        on_device, mesh=axed, in_specs=in_specs, out_specs=out_specs, check_vma=False
    )
```

profile of v0, /device:TPU:0, one launch (start us, length us, event | category | flops | bytes accessed | tf_op | source)
XLA Modules:
  0.0 241.5 jit_solution(15435969626746101923)
XLA Ops:
  0.6 3.0 %collective-permute-start.3 = (bf16[64,8192]{1,0:T(8,128)(2,1)}, bf16[64,8192]{1,0:T(8,128)(2,1)}, u32[]{:S(2)}, u32[]{:S(2)}) collective-permute-start(bf16[64,8192]{1,0:T(8,128)(2,1)} %refs_0_.3), channel_id=1, source_target_pairs={{0,2},{1,3},{2,0},{3,1},{4,5},{5,4},{6,7},{7,6},{8,10},{9,11},{10,... | collective-permute-start | bytes 3145736 | tf_op jit(solution)/shard_map/ppermute | solution.py:285
  3.7 1.5 collective-permute-start.4
  5.2 1.6 collective-permute-start
  6.8 1.4 broadcast_in_dim.82.readout
  8.1 18.8 %shard_map.131 = (bf16[1024,1024]{1,0:T(8,128)(2,1)}, f32[4,8,224]{2,1,0:T(8,128)}) custom-call(s32[1,8192]{1,0:T(1,128)} %bitcast.49, bf16[8,8192]{1,0:T(8,128)(2,1)} %broadcast_in_dim.82.readout, bf16[8192,1024]{1,0:T(8,128)(2,1)} %refs_3_.5, bf16[8192,1024]{1,0:T(8,128)(2,1)} %refs_3_.5, bf16[8192,1024]{1,0:T(8,128)(2,1)} %refs_3_.5, ...), custom_call_target="tpu_custom_call" | custom-call | flops 8589934592 | bytes 31457280 | tf_op jit(solution)/shard_map/pallas_call | solution.py:189
  28.5 1.6 gather_fusion
  31.3 2.2 collective-permute-start.6
  33.6 1.4 collective-permute-start.1
  34.9 1.3 collective-permute-start.2
  36.3 21.6 %shard_map.132 = (f32[384,128]{1,0:T(8,128)}, f32[96,128]{1,0:T(8,128)}) custom-call(bf16[64,8192]{1,0:T(8,128)(2,1)} %refs_0_.3, bf16[64,8192]{1,0:T(8,128)(2,1)} %collective-permute-done.7.refs_1_, bf16[64,8192]{1,0:T(8,128)(2,1)} %collective-permute-done.3.refs_2_, bf16[64,8192]{1,0:T(8,128)(2,1)} %collective-permute-done.8.refs_3_, ...), custom_call_target="tpu_custom_call" | custom-call | flops 11274289152 | bytes 35651584 | tf_op jit(solution)/shard_map/pallas_call | solution.py:118
  57.9 1.9 collective-permute-done.1.refs_4_
  59.8 8.6 %collective-permute-done.2.refs_6_ = bf16[64,8192]{1,0:T(8,128)(2,1)} collective-permute-done((bf16[64,8192]{1,0:T(8,128)(2,1)S(1)}, bf16[64,8192]{1,0:T(8,128)(2,1)}, u32[]{:S(2)}, u32[]{:S(2)}) %collective-permute-start.2) | collective-permute-done | bytes 1048608 | tf_op jit(solution)/shard_map/ppermute | solution.py:288
  71.3 1.4 collective-permute-done.14.refs_1_
  74.4 1.0 collective-permute-start.13
  75.4 25.1 %shard_map.133 = (f32[512,128]{1,0:T(8,128)}, f32[128,128]{1,0:T(8,128)}) custom-call(bf16[64,8192]{1,0:T(8,128)(2,1)} %collective-permute-done.5.refs_0_, bf16[64,8192]{1,0:T(8,128)(2,1)} %copy-done.18, bf16[64,8192]{1,0:T(8,128)(2,1)} %copy-done.14, bf16[64,8192]{1,0:T(8,128)(2,1)} %collective-permute-done.15.refs_3_, ...), custom_call_target="tpu_custom_call" | custom-call | flops 15032385536 | bytes 37748736 | tf_op jit(solution)/shard_map/pallas_call | solution.py:118
  100.5 6.1 %collective-permute-done.11.refs_6_ = bf16[64,8192]{1,0:T(8,128)(2,1)} collective-permute-done((bf16[64,8192]{1,0:T(8,128)(2,1)}, bf16[64,8192]{1,0:T(8,128)(2,1)}, u32[]{:S(2)}, u32[]{:S(2)}) %collective-permute-start.11) | collective-permute-done | bytes 1048608 | tf_op jit(solution)/shard_map/ppermute | solution.py:288
  108.4 1.2 collective-permute-done.22.refs_1_
  109.6 1.0 collective-permute-start.20
  111.6 1.0 collective-permute-done.25.refs_7_
  112.6 1.0 copy-done.21
  113.7 25.1 %shard_map.134 = (f32[512,128]{1,0:T(8,128)}, f32[128,128]{1,0:T(8,128)}) custom-call(bf16[64,8192]{1,0:T(8,128)(2,1)} %collective-permute-done.12.refs_0_, bf16[64,8192]{1,0:T(8,128)(2,1)} %copy-done.19, bf16[64,8192]{1,0:T(8,128)(2,1)} %collective-permute-done.6.refs_2_, bf16[64,8192]{1,0:T(8,128)(2,1)} %collective-permute-done.23.refs_3_, ...), custom_call_target="tpu_custom_call" | custom-call | flops 15032385536 | bytes 37748736 | tf_op jit(solution)/shard_map/pallas_call | solution.py:118
  138.9 5.3 %collective-permute-done.21.refs_0_ = bf16[64,8192]{1,0:T(8,128)(2,1)} collective-permute-done((bf16[64,8192]{1,0:T(8,128)(2,1)}, bf16[64,8192]{1,0:T(8,128)(2,1)}, u32[]{:S(2)}, u32[]{:S(2)}) %collective-permute-start.21) | collective-permute-done | bytes 1048608 | tf_op jit(solution)/shard_map/ppermute | solution.py:288
  145.5 2.0 collective-permute-done.26.refs_1_
  147.5 2.2 collective-permute-done.28.refs_5_
  149.7 1.8 collective-permute-done.29.refs_7_
  151.5 30.0 %shard_map.135 = (f32[640,128]{1,0:T(8,128)}, f32[160,128]{1,0:T(8,128)}) custom-call(bf16[64,8192]{1,0:T(8,128)(2,1)} %collective-permute-done.21.refs_0_, bf16[64,8192]{1,0:T(8,128)(2,1)} %collective-permute-done.26.refs_1_, bf16[64,8192]{1,0:T(8,128)(2,1)} %copy-done.15, bf16[64,8192]{1,0:T(8,128)(2,1)} %collective-permute-done.27.refs_3_, ...), custom_call_target="tpu_custom_call" | custom-call | flops 18790481920 | bytes 39845888 | tf_op jit(solution)/shard_map/pallas_call | solution.py:118
  181.5 1.0 pad_maximum_fusion
  183.2 2.1 fusion
  187.5 1.8 collective-permute-done.31
  190.9 2.5 %collective-permute-start.34 = (bf16[32,1152]{1,0:T(8,128)(2,1)S(1)}, bf16[32,1152]{1,0:T(8,128)(2,1)S(1)}, u32[]{:S(2)}, u32[]{:S(2)}) collective-permute-start(bf16[32,1152]{1,0:T(8,128)(2,1)S(1)} %concatenate.85), channel_id=1, source_target_pairs={{0,3},{1,2},{2,1},{3,0},{4,7},{5,6},{6,5},{7,4},{8,11},{9,10},{10,... | collective-permute-start | bytes 221192 | tf_op jit(solution)/shard_map/ppermute | solution.py:19
  194.0 2.3 collective-permute-done.33
  196.5 2.6 %collective-permute-start.36 = (bf16[4,8,1152]{2,1,0:T(8,128)(2,1)S(1)}, bf16[4,8,1152]{2,1,0:T(8,128)(2,1)S(1)}, u32[]{:S(2)}, u32[]{:S(2)}) collective-permute-start(bf16[4,8,1152]{2,1,0:T(8,128)(2,1)S(1)} %concatenate.86), channel_id=1, source_target_pairs={{0,16},{8,24},{16,0},{24,8},{1,17},{9,25},{17,1},{25,9},{2,18},{10... | collective-permute-start | bytes 221192 | tf_op jit(solution)/shard_map/ppermute | solution.py:24
  199.1 1.1 collective-permute-start.35
  200.2 2.7 %collective-permute-start.37 = (bf16[4,8,1152]{2,1,0:T(8,128)(2,1)S(1)}, bf16[4,8,1152]{2,1,0:T(8,128)(2,1)S(1)}, u32[]{:S(2)}, u32[]{:S(2)}) collective-permute-start(bf16[4,8,1152]{2,1,0:T(8,128)(2,1)S(1)} %concatenate.86), channel_id=1, source_target_pairs={{0,24},{8,0},{16,8},{24,16},{1,25},{9,1},{17,9},{25,17},{2,26},{10... | collective-permute-start | bytes 221192 | tf_op jit(solution)/shard_map/ppermute | solution.py:24
  202.9 2.4 collective-permute-done.35
  205.7 1.3 collective-permute-done.38
  209.3 8.4 %shard_map.136 = (bf16[16,5120]{1,0:T(8,128)(2,1)}, bf16[16,5120]{1,0:T(8,128)(2,1)}, bf16[16,5120]{1,0:T(8,128)(2,1)}, bf16[16,5120]{1,0:T(8,128)(2,1)}) custom-call(bf16[64,1024]{1,0:T(8,128)(2,1)} %subtract_convert_fusion.diff, bf16[1024,1024]{1,0:T(8,128)(2,1)} %get-tuple-element.97.refs_0_, bf16[8192,1024]{1,0:T(8,128)(2,1)} %refs_3_.5, ...), custom_call_target="tpu_custom_call" | custom-call | flops 671088640 | bytes 11141120 | tf_op jit(solution)/shard_map/pallas_call | solution.py:412
  217.7 1.5 collective-permute-start.39
  219.1 1.1 collective-permute-start.40
  220.2 1.0 collective-permute-start.41
  221.2 6.5 %shard_map.137 = (bf16[16,4096]{1,0:T(8,128)(2,1)}, bf16[16,4096]{1,0:T(8,128)(2,1)}, bf16[16,4096]{1,0:T(8,128)(2,1)}, bf16[16,4096]{1,0:T(8,128)(2,1)}) custom-call(bf16[64,1024]{1,0:T(8,128)(2,1)} %subtract_convert_fusion.diff, bf16[8192,1024]{1,0:T(8,128)(2,1)} %refs_3_.5, bf16[8192,1024]{1,0:T(8,128)(2,1)} %refs_3_.5, bf16[8192,1024]{1,0:T(8,128)(2,1)} %refs_3_.5, ...), custom_call_target="tpu_custom_call" | custom-call | flops 536870912 | bytes 8912896 | tf_op jit(solution)/shard_map/pallas_call | solution.py:412
  227.7 1.4 collective-permute-start.42
  229.2 1.1 collective-permute-start.43
  230.3 1.0 collective-permute-start.44
  231.4 4.3 %collective-permute-start.46 = (f32[16,512]{1,0:T(8,128)S(1)}, f32[16,512]{1,0:T(8,128)S(1)}, u32[]{:S(2)}, u32[]{:S(2)}) collective-permute-start(f32[16,512]{1,0:T(8,128)S(1)} %slice_add_fusion.1), channel_id=1, source_target_pairs={{0,16},{8,24},{16,0},{24,8},{1,17},{9,25},{17,1},{25,9},{2,18},{10... | collective-permute-start | bytes 98312 | tf_op jit(solution)/shard_map/ppermute | solution.py:24
  235.7 1.7 collective-permute-start.47
  237.4 1.0 convert_add_fusion.1
  238.4 1.2 collective-permute-done.47
  (176 shorter events, 21.2 us)
Async XLA Ops:
  0.6 29.5 %collective-permute-start.3 = (bf16[64,8192]{1,0:T(8,128)(2,1)}, bf16[64,8192]{1,0:T(8,128)(2,1)}, u32[]{:S(2)}, u32[]{:S(2)}) collective-permute-start(bf16[64,8192]{1,0:T(8,128)(2,1)} %refs_0_.3), channel_id=1, source_target_pairs={{0,2},{1,3},{2,0},{3,1},{4,5},{5,4},{6,7},{7,6},{8,10},{9,11},{10,... | collective-permute-start | bytes 3145736 | tf_op jit(solution)/shard_map/ppermute | solution.py:285
  3.7 26.4 %collective-permute-start.4 = (bf16[64,8192]{1,0:T(8,128)(2,1)}, bf16[64,8192]{1,0:T(8,128)(2,1)}, u32[]{:S(2)}, u32[]{:S(2)}) collective-permute-start(bf16[64,8192]{1,0:T(8,128)(2,1)} %refs_0_.3), channel_id=1, source_target_pairs={{0,1},{1,0},{2,3},{3,2},{4,6},{5,7},{6,4},{7,5},{8,9},{9,8},{10,11... | collective-permute-start | bytes 3145736 | tf_op jit(solution)/shard_map/ppermute | solution.py:288
  5.2 26.1 %collective-permute-start.7 = (bf16[64,8192]{1,0:T(8,128)(2,1)}, bf16[64,8192]{1,0:T(8,128)(2,1)}, u32[]{:S(2)}, u32[]{:S(2)}) collective-permute-start(bf16[64,8192]{1,0:T(8,128)(2,1)} %refs_0_.3), channel_id=1, source_target_pairs={{0,4},{4,0},{1,5},{5,1},{2,6},{6,2},{3,7},{7,3},{8,12},{12,8},{9,1... | collective-permute-start | bytes 3145736 | tf_op jit(solution)/shard_map/ppermute | solution.py:19
  5.2 28.4 %collective-permute-start = (bf16[64,8192]{1,0:T(8,128)(2,1)}, bf16[64,8192]{1,0:T(8,128)(2,1)S(1)}, u32[]{:S(2)}, u32[]{:S(2)}) collective-permute-start(bf16[64,8192]{1,0:T(8,128)(2,1)} %refs_0_.3), channel_id=1, source_target_pairs={{0,8},{8,16},{16,24},{24,0},{1,9},{9,17},{17,25},{25,1},{2,10},{10... | collective-permute-start | bytes 3145736 | tf_op jit(solution)/shard_map/ppermute | solution.py:24
  30.1 4.8 %collective-permute-start.8 = (bf16[64,8192]{1,0:T(8,128)(2,1)}, bf16[64,8192]{1,0:T(8,128)(2,1)}, u32[]{:S(2)}, u32[]{:S(2)}) collective-permute-start(bf16[64,8192]{1,0:T(8,128)(2,1)} %collective-permute-done.3.refs_2_), channel_id=1, source_target_pairs={{0,4},{4,0},{1,5},{5,1},{2,6},{6,2},{3,7},{7,3},{8,12},{12,8},{9,1... | collective-permute-start | bytes 3145736 | tf_op jit(solution)/shard_map/ppermute | solution.py:19
  30.3 5.9 %collective-permute-start.9 = (bf16[64,8192]{1,0:T(8,128)(2,1)}, bf16[64,8192]{1,0:T(8,128)(2,1)}, u32[]{:S(2)}, u32[]{:S(2)}) collective-permute-start(bf16[64,8192]{1,0:T(8,128)(2,1)} %collective-permute-done.4.refs_4_), channel_id=1, source_target_pairs={{0,4},{4,0},{1,5},{5,1},{2,6},{6,2},{3,7},{7,3},{8,12},{12,8},{9,1... | collective-permute-start | bytes 3145736 | tf_op jit(solution)/shard_map/ppermute | solution.py:19
  30.7 27.2 %collective-permute-start.5 = (bf16[64,8192]{1,0:T(8,128)(2,1)}, bf16[64,8192]{1,0:T(8,128)(2,1)}, u32[]{:S(2)}, u32[]{:S(2)}) collective-permute-start(bf16[64,8192]{1,0:T(8,128)(2,1)} %collective-permute-done.3.refs_2_), channel_id=1, source_target_pairs={{0,1},{1,0},{2,3},{3,2},{4,6},{5,7},{6,4},{7,5},{8,9},{9,8},{10,11... | collective-permute-start | bytes 3145736 | tf_op jit(solution)/shard_map/ppermute | solution.py:288
  31.3 26.6 %collective-permute-start.6 = (bf16[64,8192]{1,0:T(8,128)(2,1)S(1)}, bf16[64,8192]{1,0:T(8,128)(2,1)}, u32[]{:S(2)}, u32[]{:S(2)}) collective-permute-start(bf16[64,8192]{1,0:T(8,128)(2,1)S(1)} %copy-done.13), channel_id=1, source_target_pairs={{0,24},{8,0},{16,8},{24,16},{1,25},{9,1},{17,9},{25,17},{2,26},{10... | collective-permute-start | bytes 3145736 | tf_op jit(solution)/shard_map/ppermute | solution.py:24
  33.6 26.2 %collective-permute-start.1 = (bf16[64,8192]{1,0:T(8,128)(2,1)S(1)}, bf16[64,8192]{1,0:T(8,128)(2,1)}, u32[]{:S(2)}, u32[]{:S(2)}) collective-permute-start(bf16[64,8192]{1,0:T(8,128)(2,1)S(1)} %collective-permute-done.refs_2_), channel_id=1, source_target_pairs={{0,2},{1,3},{2,0},{3,1},{4,5},{5,4},{6,7},{7,6},{8,10},{9,11},{10,... | collective-permute-start | bytes 3145736 | tf_op jit(solution)/shard_map/ppermute | solution.py:285
  34.9 33.4 %collective-permute-start.2 = (bf16[64,8192]{1,0:T(8,128)(2,1)S(1)}, bf16[64,8192]{1,0:T(8,128)(2,1)}, u32[]{:S(2)}, u32[]{:S(2)}) collective-permute-start(bf16[64,8192]{1,0:T(8,128)(2,1)S(1)} %collective-permute-done.refs_2_), channel_id=1, source_target_pairs={{0,1},{1,0},{2,3},{3,2},{4,6},{5,7},{6,4},{7,5},{8,9},{9,8},{10,11... | collective-permute-start | bytes 3145736 | tf_op jit(solution)/shard_map/ppermute | solution.py:288
  36.3 37.0 %collective-permute-start.15 = (bf16[64,8192]{1,0:T(8,128)(2,1)S(1)}, bf16[64,8192]{1,0:T(8,128)(2,1)}, u32[]{:S(2)}, u32[]{:S(2)}) collective-permute-start(bf16[64,8192]{1,0:T(8,128)(2,1)S(1)} %collective-permute-done.refs_2_), channel_id=1, source_target_pairs={{0,4},{4,0},{1,5},{5,1},{2,6},{6,2},{3,7},{7,3},{8,12},{12,8},{9,1... | collective-permute-start | bytes 3145736 | tf_op jit(solution)/shard_map/ppermute | solution.py:19
  68.4 4.3 %collective-permute-start.14 = (bf16[64,8192]{1,0:T(8,128)(2,1)}, bf16[64,8192]{1,0:T(8,128)(2,1)S(1)}, u32[]{:S(2)}, u32[]{:S(2)}) collective-permute-start(bf16[64,8192]{1,0:T(8,128)(2,1)} %collective-permute-done.5.refs_0_), channel_id=1, source_target_pairs={{0,4},{4,0},{1,5},{5,1},{2,6},{6,2},{3,7},{7,3},{8,12},{12,8},{9,1... | collective-permute-start | bytes 3145736 | tf_op jit(solution)/shard_map/ppermute | solution.py:19
  68.4 5.4 %collective-permute-start.16 = (bf16[64,8192]{1,0:T(8,128)(2,1)}, bf16[64,8192]{1,0:T(8,128)(2,1)}, u32[]{:S(2)}, u32[]{:S(2)}) collective-permute-start(bf16[64,8192]{1,0:T(8,128)(2,1)} %collective-permute-done.1.refs_4_), channel_id=1, source_target_pairs={{0,4},{4,0},{1,5},{5,1},{2,6},{6,2},{3,7},{7,3},{8,12},{12,8},{9,1... | collective-permute-start | bytes 3145736 | tf_op jit(solution)/shard_map/ppermute | solution.py:19
  68.9 5.5 %collective-permute-start.17 = (bf16[64,8192]{1,0:T(8,128)(2,1)}, bf16[64,8192]{1,0:T(8,128)(2,1)}, u32[]{:S(2)}, u32[]{:S(2)}) collective-permute-start(bf16[64,8192]{1,0:T(8,128)(2,1)} %collective-permute-done.2.refs_6_), channel_id=1, source_target_pairs={{0,4},{4,0},{1,5},{5,1},{2,6},{6,2},{3,7},{7,3},{8,12},{12,8},{9,1... | collective-permute-start | bytes 3145736 | tf_op jit(solution)/shard_map/ppermute | solution.py:19
  69.0 31.5 %collective-permute-start.12 = (bf16[64,8192]{1,0:T(8,128)(2,1)}, bf16[64,8192]{1,0:T(8,128)(2,1)}, u32[]{:S(2)}, u32[]{:S(2)}) collective-permute-start(bf16[64,8192]{1,0:T(8,128)(2,1)} %collective-permute-done.1.refs_4_), channel_id=1, source_target_pairs={{0,1},{1,0},{2,3},{3,2},{4,6},{5,7},{6,4},{7,5},{8,9},{9,8},{10,11... | collective-permute-start | bytes 3145736 | tf_op jit(solution)/shard_map/ppermute | solution.py:288
  72.7 27.8 %collective-permute-start.10 = (bf16[64,8192]{1,0:T(8,128)(2,1)}, bf16[64,8192]{1,0:T(8,128)(2,1)}, u32[]{:S(2)}, u32[]{:S(2)}) collective-permute-start(bf16[64,8192]{1,0:T(8,128)(2,1)} %collective-permute-done.6.refs_2_), channel_id=1, source_target_pairs={{0,2},{1,3},{2,0},{3,1},{4,5},{5,4},{6,7},{7,6},{8,10},{9,11},{10,... | collective-permute-start | bytes 3145736 | tf_op jit(solution)/shard_map/ppermute | solution.py:285
  73.2 33.4 %collective-permute-start.11 = (bf16[64,8192]{1,0:T(8,128)(2,1)}, bf16[64,8192]{1,0:T(8,128)(2,1)}, u32[]{:S(2)}, u32[]{:S(2)}) collective-permute-start(bf16[64,8192]{1,0:T(8,128)(2,1)} %collective-permute-done.6.refs_2_), channel_id=1, source_target_pairs={{0,1},{1,0},{2,3},{3,2},{4,6},{5,7},{6,4},{7,5},{8,9},{9,8},{10,11... | collective-permute-start | bytes 3145736 | tf_op jit(solution)/shard_map/ppermute | solution.py:288
  73.7 34.1 %collective-permute-start.23 = (bf16[64,8192]{1,0:T(8,128)(2,1)}, bf16[64,8192]{1,0:T(8,128)(2,1)}, u32[]{:S(2)}, u32[]{:S(2)}) collective-permute-start(bf16[64,8192]{1,0:T(8,128)(2,1)} %collective-permute-done.6.refs_2_), channel_id=1, source_target_pairs={{0,4},{4,0},{1,5},{5,1},{2,6},{6,2},{3,7},{7,3},{8,12},{12,8},{9,1... | collective-permute-start | bytes 3145736 | tf_op jit(solution)/shard_map/ppermute | solution.py:19
  74.4 32.3 %collective-permute-start.13 = (bf16[64,8192]{1,0:T(8,128)(2,1)S(1)}, bf16[64,8192]{1,0:T(8,128)(2,1)S(1)}, u32[]{:S(2)}, u32[]{:S(2)}) collective-permute-start(bf16[64,8192]{1,0:T(8,128)(2,1)S(1)} %collective-permute-done.refs_2_), channel_id=1, source_target_pairs={{0,8},{8,16},{16,24},{24,0},{1,9},{9,17},{17,25},{25,1},{2,10},{10... | collective-permute-start | bytes 3145736 | tf_op jit(solution)/shard_map/ppermute | solution.py:24
  106.7 2.9 %collective-permute-start.22 = (bf16[64,8192]{1,0:T(8,128)(2,1)}, bf16[64,8192]{1,0:T(8,128)(2,1)S(1)}, u32[]{:S(2)}, u32[]{:S(2)}) collective-permute-start(bf16[64,8192]{1,0:T(8,128)(2,1)} %collective-permute-done.12.refs_0_), channel_id=1, source_target_pairs={{0,4},{4,0},{1,5},{5,1},{2,6},{6,2},{3,7},{7,3},{8,12},{12,8},{9,1... | collective-permute-start | bytes 3145736 | tf_op jit(solution)/shard_map/ppermute | solution.py:19
  106.7 4.4 %collective-permute-start.24 = (bf16[64,8192]{1,0:T(8,128)(2,1)}, bf16[64,8192]{1,0:T(8,128)(2,1)S(1)}, u32[]{:S(2)}, u32[]{:S(2)}) collective-permute-start(bf16[64,8192]{1,0:T(8,128)(2,1)} %collective-permute-done.10.refs_4_), channel_id=1, source_target_pairs={{0,4},{4,0},{1,5},{5,1},{2,6},{6,2},{3,7},{7,3},{8,12},{12,8},{9,1... | collective-permute-start | bytes 3145736 | tf_op jit(solution)/shard_map/ppermute | solution.py:19
  107.2 5.4 %collective-permute-start.25 = (bf16[64,8192]{1,0:T(8,128)(2,1)}, bf16[64,8192]{1,0:T(8,128)(2,1)S(1)}, u32[]{:S(2)}, u32[]{:S(2)}) collective-permute-start(bf16[64,8192]{1,0:T(8,128)(2,1)} %collective-permute-done.11.refs_6_), channel_id=1, source_target_pairs={{0,4},{4,0},{1,5},{5,1},{2,6},{6,2},{3,7},{7,3},{8,12},{12,8},{9,1... | collective-permute-start | bytes 3145736 | tf_op jit(solution)/shard_map/ppermute | solution.py:19
  107.3 31.5 %collective-permute-start.18 = (bf16[64,8192]{1,0:T(8,128)(2,1)S(1)}, bf16[64,8192]{1,0:T(8,128)(2,1)S(1)}, u32[]{:S(2)}, u32[]{:S(2)}) collective-permute-start(bf16[64,8192]{1,0:T(8,128)(2,1)S(1)} %collective-permute-done.13.refs_2_), channel_id=1, source_target_pairs={{0,2},{1,3},{2,0},{3,1},{4,5},{5,4},{6,7},{7,6},{8,10},{9,11},{10,... | collective-permute-start | bytes 3145736 | tf_op jit(solution)/shard_map/ppermute | solution.py:285
  107.8 31.0 %collective-permute-start.19 = (bf16[64,8192]{1,0:T(8,128)(2,1)S(1)}, bf16[64,8192]{1,0:T(8,128)(2,1)S(1)}, u32[]{:S(2)}, u32[]{:S(2)}) collective-permute-start(bf16[64,8192]{1,0:T(8,128)(2,1)S(1)} %collective-permute-done.13.refs_2_), channel_id=1, source_target_pairs={{0,1},{1,0},{2,3},{3,2},{4,6},{5,7},{6,4},{7,5},{8,9},{9,8},{10,11... | collective-permute-start | bytes 3145736 | tf_op jit(solution)/shard_map/ppermute | solution.py:288
  109.6 29.3 %collective-permute-start.20 = (bf16[64,8192]{1,0:T(8,128)(2,1)}, bf16[64,8192]{1,0:T(8,128)(2,1)}, u32[]{:S(2)}, u32[]{:S(2)}) collective-permute-start(bf16[64,8192]{1,0:T(8,128)(2,1)} %collective-permute-done.12.refs_0_), channel_id=1, source_target_pairs={{0,8},{8,16},{16,24},{24,0},{1,9},{9,17},{17,25},{25,1},{2,10},{10... | collective-permute-start | bytes 3145736 | tf_op jit(solution)/shard_map/ppermute | solution.py:24
  111.1 33.1 %collective-permute-start.21 = (bf16[64,8192]{1,0:T(8,128)(2,1)}, bf16[64,8192]{1,0:T(8,128)(2,1)}, u32[]{:S(2)}, u32[]{:S(2)}) collective-permute-start(bf16[64,8192]{1,0:T(8,128)(2,1)} %collective-permute-done.10.refs_4_), channel_id=1, source_target_pairs={{0,1},{1,0},{2,3},{3,2},{4,6},{5,7},{6,4},{7,5},{8,9},{9,8},{10,11... | collective-permute-start | bytes 3145736 | tf_op jit(solution)/shard_map/ppermute | solution.py:288
  113.6 31.9 %collective-permute-start.27 = (bf16[64,8192]{1,0:T(8,128)(2,1)S(1)}, bf16[64,8192]{1,0:T(8,128)(2,1)}, u32[]{:S(2)}, u32[]{:S(2)}) collective-permute-start(bf16[64,8192]{1,0:T(8,128)(2,1)S(1)} %collective-permute-done.13.refs_2_), channel_id=1, source_target_pairs={{0,4},{4,0},{1,5},{5,1},{2,6},{6,2},{3,7},{7,3},{8,12},{12,8},{9,1... | collective-permute-start | bytes 3145736 | tf_op jit(solution)/shard_map/ppermute | solution.py:19
  144.1 3.3 %collective-permute-start.26 = (bf16[64,8192]{1,0:T(8,128)(2,1)}, bf16[64,8192]{1,0:T(8,128)(2,1)}, u32[]{:S(2)}, u32[]{:S(2)}) collective-permute-start(bf16[64,8192]{1,0:T(8,128)(2,1)} %collective-permute-done.21.refs_0_), channel_id=1, source_target_pairs={{0,4},{4,0},{1,5},{5,1},{2,6},{6,2},{3,7},{7,3},{8,12},{12,8},{9,1... | collective-permute-start | bytes 3145736 | tf_op jit(solution)/shard_map/ppermute | solution.py:19
  144.3 5.4 %collective-permute-start.28 = (bf16[64,8192]{1,0:T(8,128)(2,1)S(1)}, bf16[64,8192]{1,0:T(8,128)(2,1)}, u32[]{:S(2)}, u32[]{:S(2)}) collective-permute-start(bf16[64,8192]{1,0:T(8,128)(2,1)S(1)} %collective-permute-done.18.refs_4_), channel_id=1, source_target_pairs={{0,4},{4,0},{1,5},{5,1},{2,6},{6,2},{3,7},{7,3},{8,12},{12,8},{9,1... | collective-permute-start | bytes 3145736 | tf_op jit(solution)/shard_map/ppermute | solution.py:19
  144.7 6.8 %collective-permute-start.29 = (bf16[64,8192]{1,0:T(8,128)(2,1)S(1)}, bf16[64,8192]{1,0:T(8,128)(2,1)}, u32[]{:S(2)}, u32[]{:S(2)}) collective-permute-start(bf16[64,8192]{1,0:T(8,128)(2,1)S(1)} %collective-permute-done.19.refs_6_), channel_id=1, source_target_pairs={{0,4},{4,0},{1,5},{5,1},{2,6},{6,2},{3,7},{7,3},{8,12},{12,8},{9,1... | collective-permute-start | bytes 3145736 | tf_op jit(solution)/shard_map/ppermute | solution.py:19
  144.8 6.7 %collective-permute-start.30 = (bf16[64,8192]{1,0:T(8,128)(2,1)}, bf16[64,8192]{1,0:T(8,128)(2,1)}, u32[]{:S(2)}, u32[]{:S(2)}) collective-permute-start(bf16[64,8192]{1,0:T(8,128)(2,1)} %collective-permute-done.20.refs_8_), channel_id=1, source_target_pairs={{0,4},{4,0},{1,5},{5,1},{2,6},{6,2},{3,7},{7,3},{8,12},{12,8},{9,1... | collective-permute-start | bytes 3145736 | tf_op jit(solution)/shard_map/ppermute | solution.py:19
  187.3 2.0 collective-permute-start.31
  189.6 4.4 %collective-permute-start.32 = (bf16[32,1152]{1,0:T(8,128)(2,1)S(1)}, bf16[32,1152]{1,0:T(8,128)(2,1)S(1)}, u32[]{:S(2)}, u32[]{:S(2)}) collective-permute-start(bf16[32,1152]{1,0:T(8,128)(2,1)S(1)} %concatenate.83), channel_id=1, source_target_pairs={{0,1},{1,0},{2,3},{3,2},{4,5},{5,4},{6,7},{7,6},{8,9},{9,8},{10,11... | collective-permute-start | bytes 221192 | tf_op jit(solution)/shard_map/ppermute | solution.py:19
  190.3 6.0 %collective-permute-start.33 = (bf16[32,1152]{1,0:T(8,128)(2,1)S(1)}, bf16[32,1152]{1,0:T(8,128)(2,1)S(1)}, u32[]{:S(2)}, u32[]{:S(2)}) collective-permute-start(bf16[32,1152]{1,0:T(8,128)(2,1)S(1)} %concatenate.84), channel_id=1, source_target_pairs={{0,2},{1,3},{2,0},{3,1},{4,6},{5,7},{6,4},{7,5},{8,10},{9,11},{10,... | collective-permute-start | bytes 221192 | tf_op jit(solution)/shard_map/ppermute | solution.py:19
  190.9 5.4 %collective-permute-start.34 = (bf16[32,1152]{1,0:T(8,128)(2,1)S(1)}, bf16[32,1152]{1,0:T(8,128)(2,1)S(1)}, u32[]{:S(2)}, u32[]{:S(2)}) collective-permute-start(bf16[32,1152]{1,0:T(8,128)(2,1)S(1)} %concatenate.85), channel_id=1, source_target_pairs={{0,3},{1,2},{2,1},{3,0},{4,7},{5,6},{6,5},{7,4},{8,11},{9,10},{10,... | collective-permute-start | bytes 221192 | tf_op jit(solution)/shard_map/ppermute | solution.py:19
  196.5 8.9 %collective-permute-start.36 = (bf16[4,8,1152]{2,1,0:T(8,128)(2,1)S(1)}, bf16[4,8,1152]{2,1,0:T(8,128)(2,1)S(1)}, u32[]{:S(2)}, u32[]{:S(2)}) collective-permute-start(bf16[4,8,1152]{2,1,0:T(8,128)(2,1)S(1)} %concatenate.86), channel_id=1, source_target_pairs={{0,16},{8,24},{16,0},{24,8},{1,17},{9,25},{17,1},{25,9},{2,18},{10... | collective-permute-start | bytes 221192 | tf_op jit(solution)/shard_map/ppermute | solution.py:24
  199.1 6.2 %collective-permute-start.35 = (bf16[4,8,1152]{2,1,0:T(8,128)(2,1)S(1)}, bf16[4,8,1152]{2,1,0:T(8,128)(2,1)S(1)}, u32[]{:S(2)}, u32[]{:S(2)}) collective-permute-start(bf16[4,8,1152]{2,1,0:T(8,128)(2,1)S(1)} %concatenate.86), channel_id=1, source_target_pairs={{0,8},{8,16},{16,24},{24,0},{1,9},{9,17},{17,25},{25,1},{2,10},{10... | collective-permute-start | bytes 221192 | tf_op jit(solution)/shard_map/ppermute | solution.py:24
  200.2 5.2 %collective-permute-start.37 = (bf16[4,8,1152]{2,1,0:T(8,128)(2,1)S(1)}, bf16[4,8,1152]{2,1,0:T(8,128)(2,1)S(1)}, u32[]{:S(2)}, u32[]{:S(2)}) collective-permute-start(bf16[4,8,1152]{2,1,0:T(8,128)(2,1)S(1)} %concatenate.86), channel_id=1, source_target_pairs={{0,24},{8,0},{16,8},{24,16},{1,25},{9,1},{17,9},{25,17},{2,26},{10... | collective-permute-start | bytes 221192 | tf_op jit(solution)/shard_map/ppermute | solution.py:24
  205.6 1.4 collective-permute-start.38
  217.7 12.6 %collective-permute-start.39 = (bf16[16,5120]{1,0:T(8,128)(2,1)}, bf16[16,5120]{1,0:T(8,128)(2,1)S(1)}, u32[]{:S(2)}, u32[]{:S(2)}) collective-permute-start(bf16[16,5120]{1,0:T(8,128)(2,1)} %get-tuple-element.99), channel_id=1, source_target_pairs={{0,1},{1,0},{2,3},{3,2},{4,5},{5,4},{6,7},{7,6},{8,9},{9,8},{10,11... | collective-permute-start | bytes 491528 | tf_op jit(solution)/shard_map/ppermute | solution.py:19
  219.1 12.1 %collective-permute-start.40 = (bf16[16,5120]{1,0:T(8,128)(2,1)}, bf16[16,5120]{1,0:T(8,128)(2,1)S(1)}, u32[]{:S(2)}, u32[]{:S(2)}) collective-permute-start(bf16[16,5120]{1,0:T(8,128)(2,1)} %get-tuple-element.100), channel_id=1, source_target_pairs={{0,2},{1,3},{2,0},{3,1},{4,6},{5,7},{6,4},{7,5},{8,10},{9,11},{10,... | collective-permute-start | bytes 491528 | tf_op jit(solution)/shard_map/ppermute | solution.py:19
  220.2 11.0 %collective-permute-start.41 = (bf16[16,5120]{1,0:T(8,128)(2,1)}, bf16[16,5120]{1,0:T(8,128)(2,1)S(1)}, u32[]{:S(2)}, u32[]{:S(2)}) collective-permute-start(bf16[16,5120]{1,0:T(8,128)(2,1)} %get-tuple-element.101), channel_id=1, source_target_pairs={{0,3},{1,2},{2,1},{3,0},{4,7},{5,6},{6,5},{7,4},{8,11},{9,10},{10,... | collective-permute-start | bytes 491528 | tf_op jit(solution)/shard_map/ppermute | solution.py:19
  227.7 8.0 %collective-permute-start.42 = (bf16[16,4096]{1,0:T(8,128)(2,1)}, bf16[16,4096]{1,0:T(8,128)(2,1)S(1)}, u32[]{:S(2)}, u32[]{:S(2)}) collective-permute-start(bf16[16,4096]{1,0:T(8,128)(2,1)} %get-tuple-element.103), channel_id=1, source_target_pairs={{0,1},{1,0},{2,3},{3,2},{4,5},{5,4},{6,7},{7,6},{8,9},{9,8},{10,11... | collective-permute-start | bytes 393224 | tf_op jit(solution)/shard_map/ppermute | solution.py:19
  229.2 8.2 %collective-permute-start.43 = (bf16[16,4096]{1,0:T(8,128)(2,1)}, bf16[16,4096]{1,0:T(8,128)(2,1)S(1)}, u32[]{:S(2)}, u32[]{:S(2)}) collective-permute-start(bf16[16,4096]{1,0:T(8,128)(2,1)} %get-tuple-element.104), channel_id=1, source_target_pairs={{0,2},{1,3},{2,0},{3,1},{4,6},{5,7},{6,4},{7,5},{8,10},{9,11},{10,... | collective-permute-start | bytes 393224 | tf_op jit(solution)/shard_map/ppermute | solution.py:19
  230.3 7.1 %collective-permute-start.44 = (bf16[16,4096]{1,0:T(8,128)(2,1)}, bf16[16,4096]{1,0:T(8,128)(2,1)S(1)}, u32[]{:S(2)}, u32[]{:S(2)}) collective-permute-start(bf16[16,4096]{1,0:T(8,128)(2,1)} %get-tuple-element.105), channel_id=1, source_target_pairs={{0,3},{1,2},{2,1},{3,0},{4,7},{5,6},{6,5},{7,4},{8,11},{9,10},{10,... | collective-permute-start | bytes 393224 | tf_op jit(solution)/shard_map/ppermute | solution.py:19
  231.4 7.0 %collective-permute-start.45 = (f32[16,512]{1,0:T(8,128)S(1)}, f32[16,512]{1,0:T(8,128)S(1)}, u32[]{:S(2)}, u32[]{:S(2)}) collective-permute-start(f32[16,512]{1,0:T(8,128)S(1)} %slice_add_fusion.1), channel_id=1, source_target_pairs={{0,8},{8,16},{16,24},{24,0},{1,9},{9,17},{17,25},{25,1},{2,10},{10... | collective-permute-start | bytes 98312 | tf_op jit(solution)/shard_map/ppermute | solution.py:24
  231.4 6.9 %collective-permute-start.46 = (f32[16,512]{1,0:T(8,128)S(1)}, f32[16,512]{1,0:T(8,128)S(1)}, u32[]{:S(2)}, u32[]{:S(2)}) collective-permute-start(f32[16,512]{1,0:T(8,128)S(1)} %slice_add_fusion.1), channel_id=1, source_target_pairs={{0,16},{8,24},{16,0},{24,8},{1,17},{9,25},{17,1},{25,9},{2,18},{10... | collective-permute-start | bytes 98312 | tf_op jit(solution)/shard_map/ppermute | solution.py:24
  235.7 3.9 %collective-permute-start.47 = (f32[16,512]{1,0:T(8,128)S(1)}, f32[16,512]{1,0:T(8,128)S(1)}, u32[]{:S(2)}, u32[]{:S(2)}) collective-permute-start(f32[16,512]{1,0:T(8,128)S(1)} %slice_add_fusion.1), channel_id=1, source_target_pairs={{0,24},{8,0},{16,8},{24,16},{1,25},{9,1},{17,9},{25,17},{2,26},{10... | collective-permute-start | bytes 98312 | tf_op jit(solution)/shard_map/ppermute | solution.py:24
  (23 other events, 397.4 us)
where the time goes:
time: 242 us
  Pallas kernels  136 us (56%)
  starting transfers between devices  43.1 us (18%)
  waiting for transfers between devices  42.5 us (18%)
  local copies, waits for them, and re-layouts  11.5 us (5%)
  other arithmetic  5.52 us (2%)
    pallas_call x4, Pallas kernels, layer(): pl.pallas_call(functools.partial(layer_kernel, count, length), grid=(dept...  102 us
    ppermute x7, waiting for transfers between devices, send_b(): return lax.ppermute(value, plane, plane_perm(second))  20 us
    pallas_call x1, Pallas kernels, prepare(): pl.pallas_call(prepare_kernel, grid=(steps,), in_specs=[pl.BlockSpec((1,...  18.8 us
    ppermute x10, starting transfers between devices, turn(): lax.ppermute(value, axis, [(i, (i + shift) % size) for i in range(size)])  18.3 us
    ppermute x28, waiting for transfers between devices, swap(): return lax.ppermute(value, axis, [(i, i ^ mask) for i in range(size)])  17 us
    pallas_call x2, Pallas kernels, contrast_parts(): pl.pallas_call(functools.partial(contrast_kernel, table is not None), gri...  14.9 us
    ppermute x28, starting transfers between devices, swap(): return lax.ppermute(value, axis, [(i, i ^ mask) for i in range(size)])  13.8 us
    ppermute x7, starting transfers between devices, send_b(): return lax.ppermute(value, plane, plane_perm(second))  5.59 us
  transfers between devices with their start and end apart: 49, of which 19 were waited for; matrix products, arithmetic and copies ran while one was open for 4% of the time, Pallas kernels for 40%

commit v1 on v0

--- a/solution.py
+++ b/solution.py
@@ -290,8 +290,9 @@
     def ring(value, shift=1):
         return turn(value, "chip", shift)
 
-    sin = sketch_in.reshape(parts, kin // parts, -1)[jnp.arange(parts) ^ pd]
-    sin = sin.reshape(sketch_in.shape)
+    def reorder(sketch_in):
+        by_part = sketch_in.reshape(parts, kin // parts, -1)
+        return by_part[jnp.arange(parts) ^ pd].reshape(sketch_in.shape)
 
     def run(*pieces):
         return layer(pieces, gate_weight, up_weight, sin, sketch_out, wvec, length)
@@ -299,12 +300,13 @@
     p0 = states
     p0s = sibling(p0)
     a0, b0, p1 = send_a(p0), send_b(p0), ring(p0)
-    a0, b0, table, wvec, sin = tie((a0, b0, table, wvec, sin))
+    a0, b0, p1, table = tie((a0, b0, p1, table))
+    a1, b1, d0 = send_a(p1), send_b(p1), send_b(a0)
+    sketch_in, wvec, _ = tie((sketch_in, wvec, a0))
+    sin = reorder(sketch_in)
     a0, p0 = tie((a0, p0))
     p3 = ring(p0, -1)
     a0s, b0s = sibling(a0), sibling(b0)
-    a1, b1 = send_a(p1), send_b(p1)
-    d0 = send_b(a0)
     out0 = run(p0, p0s, a0, a0s, b0, b0s)
     extras = extras(out0[1])
     p1s = sibling(p1)

time: 242 us -> 243 us (level)
  waiting for transfers between devices: 42.5 us -> 45.3 us
    ppermute x10, waiting for transfers between devices: 3.65 us -> 10.3 us  [turn(): lax.ppermute(value, axis, [(i, (i + shift) % size) for i in range(size)])]
    ppermute x10, starting transfers between devices: 18.3 us -> 13.6 us  [turn(): lax.ppermute(value, axis, [(i, (i + shift) % size) for i in range(size)])]
    ppermute x7, starting transfers between devices: 5.59 us -> 8.7 us  [send_b(): return lax.ppermute(value, plane, plane_perm(second))]
  transfers between devices with their start and end apart: 49 -> 49, of which waited for: 19 -> 22; matrix products, arithmetic and copies ran while one was open for 4% -> 4% of each run, Pallas kernels for 40% -> 40%
where the time goes in v1:
time: 243 us; the launch traced here: 242 us
  Pallas kernels  136 us (56%)
  waiting for transfers between devices  45.3 us (19%)
  starting transfers between devices  41.2 us (17%)
  local copies, waits for them, and re-layouts  11.4 us (5%)
  other arithmetic  5.51 us (2%)
    pallas_call x4, Pallas kernels, layer(): pl.pallas_call(functools.partial(layer_kernel, count, length), grid=(dept...  102 us
    ppermute x7, waiting for transfers between devices, send_b(): return lax.ppermute(value, plane, plane_perm(second))  19.1 us
    pallas_call x1, Pallas kernels, prepare(): pl.pallas_call(prepare_kernel, grid=(steps,), in_specs=[pl.BlockSpec((1,...  18.8 us
    ppermute x28, waiting for transfers between devices, swap(): return lax.ppermute(value, axis, [(i, i ^ mask) for i in range(size)])  15.3 us
    pallas_call x2, Pallas kernels, contrast_parts(): pl.pallas_call(functools.partial(contrast_kernel, table is not None), gri...  14.9 us
    ppermute x28, starting transfers between devices, swap(): return lax.ppermute(value, axis, [(i, i ^ mask) for i in range(size)])  14.2 us
    ppermute x10, starting transfers between devices, turn(): lax.ppermute(value, axis, [(i, (i + shift) % size) for i in range(size)])  13.6 us
    ppermute x10, waiting for transfers between devices, turn(): lax.ppermute(value, axis, [(i, (i + shift) % size) for i in range(size)])  10.3 us
  transfers between devices with their start and end apart: 49, of which 22 were waited for; matrix products, arithmetic and copies ran while one was open for 4% of the time, Pallas kernels for 40%

profile of v1, /device:TPU:0, one launch (start us, length us, event | category | flops | bytes accessed | tf_op | source)
XLA Modules:
  0.0 242.2 jit_solution(15344107053781309301)
XLA Ops:
  0.6 3.0 %collective-permute-start = (bf16[64,8192]{1,0:T(8,128)(2,1)}, bf16[64,8192]{1,0:T(8,128)(2,1)}, u32[]{:S(2)}, u32[]{:S(2)}) collective-permute-start(bf16[64,8192]{1,0:T(8,128)(2,1)} %refs_0_.3), channel_id=1, source_target_pairs={{0,2},{1,3},{2,0},{3,1},{4,5},{5,4},{6,7},{7,6},{8,10},{9,11},{10,... | collective-permute-start | bytes 3145736 | tf_op jit(solution)/shard_map/ppermute | solution.py:285
  3.7 1.5 collective-permute-start.1
  5.2 1.6 collective-permute-start.2
  6.8 1.4 broadcast_in_dim.82.readout
  8.1 18.8 %shard_map.131 = (bf16[1024,1024]{1,0:T(8,128)(2,1)}, f32[4,8,224]{2,1,0:T(8,128)}) custom-call(s32[1,8192]{1,0:T(1,128)} %bitcast.49, bf16[8,8192]{1,0:T(8,128)(2,1)} %broadcast_in_dim.82.readout, bf16[8192,1024]{1,0:T(8,128)(2,1)} %refs_3_.5, bf16[8192,1024]{1,0:T(8,128)(2,1)} %refs_3_.5, bf16[8192,1024]{1,0:T(8,128)(2,1)} %refs_3_.5, ...), custom_call_target="tpu_custom_call" | custom-call | flops 8589934592 | bytes 31457280 | tf_op jit(solution)/shard_map/pallas_call | solution.py:189
  27.5 4.1 %collective-permute-done.2.refs_2_ = bf16[64,8192]{1,0:T(8,128)(2,1)S(1)} collective-permute-done((bf16[64,8192]{1,0:T(8,128)(2,1)}, bf16[64,8192]{1,0:T(8,128)(2,1)S(1)}, u32[]{:S(2)}, u32[]{:S(2)}) %collective-permute-start.2) | collective-permute-done | bytes 1048608 | tf_op jit(solution)/shard_map/ppermute | solution.py:24
  34.8 1.6 gather_fusion
  36.4 1.5 collective-permute-start.5
  37.9 1.8 collective-permute-start.6
  39.6 21.6 %shard_map.132 = (f32[384,128]{1,0:T(8,128)}, f32[96,128]{1,0:T(8,128)}) custom-call(bf16[64,8192]{1,0:T(8,128)(2,1)} %refs_0_.3, bf16[64,8192]{1,0:T(8,128)(2,1)} %collective-permute-done.7.refs_1_, bf16[64,8192]{1,0:T(8,128)(2,1)} %collective-permute-done.refs_2_, bf16[64,8192]{1,0:T(8,128)(2,1)} %collective-permute-done.8.refs_3_, ...), custom_call_target="tpu_custom_call" | custom-call | flops 11274289152 | bytes 35651584 | tf_op jit(solution)/shard_map/pallas_call | solution.py:118
  61.3 2.3 collective-permute-done.6.refs_2_
  63.6 6.6 %collective-permute-done.5.refs_0_ = bf16[64,8192]{1,0:T(8,128)(2,1)} collective-permute-done((bf16[64,8192]{1,0:T(8,128)(2,1)}, bf16[64,8192]{1,0:T(8,128)(2,1)}, u32[]{:S(2)}, u32[]{:S(2)}) %collective-permute-start.5) | collective-permute-done | bytes 1048608 | tf_op jit(solution)/shard_map/ppermute | solution.py:288
  70.9 1.3 collective-permute-start.12
  74.4 1.5 collective-permute-start.11
  76.1 25.1 %shard_map.133 = (f32[512,128]{1,0:T(8,128)}, f32[128,128]{1,0:T(8,128)}) custom-call(bf16[64,8192]{1,0:T(8,128)(2,1)} %collective-permute-done.5.refs_0_, bf16[64,8192]{1,0:T(8,128)(2,1)} %copy-done.18, bf16[64,8192]{1,0:T(8,128)(2,1)} %copy-done.14, bf16[64,8192]{1,0:T(8,128)(2,1)} %collective-permute-done.15.refs_3_, ...), custom_call_target="tpu_custom_call" | custom-call | flops 15032385536 | bytes 37748736 | tf_op jit(solution)/shard_map/pallas_call | solution.py:118
  101.3 7.2 %collective-permute-done.11.refs_6_ = bf16[64,8192]{1,0:T(8,128)(2,1)} collective-permute-done((bf16[64,8192]{1,0:T(8,128)(2,1)}, bf16[64,8192]{1,0:T(8,128)(2,1)}, u32[]{:S(2)}, u32[]{:S(2)}) %collective-permute-start.11) | collective-permute-done | bytes 1048608 | tf_op jit(solution)/shard_map/ppermute | solution.py:288
  109.7 1.2 collective-permute-start.19
  111.5 1.5 collective-permute-done.24.refs_5_
  113.0 1.2 collective-permute-start.21
  114.5 1.0 copy-done.21
  115.6 25.1 %shard_map.134 = (f32[512,128]{1,0:T(8,128)}, f32[128,128]{1,0:T(8,128)}) custom-call(bf16[64,8192]{1,0:T(8,128)(2,1)} %collective-permute-done.12.refs_0_, bf16[64,8192]{1,0:T(8,128)(2,1)} %copy-done.19, bf16[64,8192]{1,0:T(8,128)(2,1)} %collective-permute-done.6.refs_2_, bf16[64,8192]{1,0:T(8,128)(2,1)} %collective-permute-done.23.refs_3_, ...), custom_call_target="tpu_custom_call" | custom-call | flops 15032385536 | bytes 37748736 | tf_op jit(solution)/shard_map/pallas_call | solution.py:118
  140.7 5.3 %collective-permute-done.21.refs_0_ = bf16[64,8192]{1,0:T(8,128)(2,1)} collective-permute-done((bf16[64,8192]{1,0:T(8,128)(2,1)}, bf16[64,8192]{1,0:T(8,128)(2,1)}, u32[]{:S(2)}, u32[]{:S(2)}) %collective-permute-start.21) | collective-permute-done | bytes 1048608 | tf_op jit(solution)/shard_map/ppermute | solution.py:288
  147.4 1.6 collective-permute-done.26.refs_1_
  149.0 2.8 %collective-permute-done.28.refs_5_ = bf16[64,8192]{1,0:T(8,128)(2,1)} collective-permute-done((bf16[64,8192]{1,0:T(8,128)(2,1)S(1)}, bf16[64,8192]{1,0:T(8,128)(2,1)}, u32[]{:S(2)}, u32[]{:S(2)}) %collective-permute-start.28) | collective-permute-done | bytes 1048608 | tf_op jit(solution)/shard_map/ppermute | solution.py:19
  151.8 1.5 collective-permute-done.29.refs_7_
  153.3 30.0 %shard_map.135 = (f32[640,128]{1,0:T(8,128)}, f32[160,128]{1,0:T(8,128)}) custom-call(bf16[64,8192]{1,0:T(8,128)(2,1)} %collective-permute-done.21.refs_0_, bf16[64,8192]{1,0:T(8,128)(2,1)} %collective-permute-done.26.refs_1_, bf16[64,8192]{1,0:T(8,128)(2,1)} %copy-done.15, bf16[64,8192]{1,0:T(8,128)(2,1)} %collective-permute-done.27.refs_3_, ...), custom_call_target="tpu_custom_call" | custom-call | flops 18790481920 | bytes 39845888 | tf_op jit(solution)/shard_map/pallas_call | solution.py:118
  183.3 1.0 pad_maximum_fusion
  185.0 2.1 fusion
  189.6 1.6 collective-permute-done.31
  191.4 1.3 collective-permute-start.32
  193.5 1.8 collective-permute-start.34
  196.0 2.2 collective-permute-done.33
  199.8 1.5 collective-permute-start.35
  201.3 2.3 collective-permute-start.37
  203.6 2.5 %collective-permute-done.35 = bf16[4,8,1152]{2,1,0:T(8,128)(2,1)S(1)} collective-permute-done((bf16[4,8,1152]{2,1,0:T(8,128)(2,1)S(1)}, bf16[4,8,1152]{2,1,0:T(8,128)(2,1)S(1)}, u32[]{:S(2)}, u32[]{:S(2)}) %collective-permute-start.35) | collective-permute-done | bytes 73760 | tf_op jit(solution)/shard_map/ppermute | solution.py:24
  206.1 0.9 collective-permute-done.37
  207.3 1.3 collective-permute-done.38
  210.9 8.4 %shard_map.136 = (bf16[16,5120]{1,0:T(8,128)(2,1)}, bf16[16,5120]{1,0:T(8,128)(2,1)}, bf16[16,5120]{1,0:T(8,128)(2,1)}, bf16[16,5120]{1,0:T(8,128)(2,1)}) custom-call(bf16[64,1024]{1,0:T(8,128)(2,1)} %subtract_convert_fusion.diff, bf16[1024,1024]{1,0:T(8,128)(2,1)} %get-tuple-element.99.refs_0_, bf16[8192,1024]{1,0:T(8,128)(2,1)} %refs_3_.5, ...), custom_call_target="tpu_custom_call" | custom-call | flops 671088640 | bytes 11141120 | tf_op jit(solution)/shard_map/pallas_call | solution.py:414
  219.3 0.8 collective-permute-start.39
  220.1 1.5 collective-permute-start.40
  221.6 1.2 collective-permute-start.41
  222.8 6.5 %shard_map.137 = (bf16[16,4096]{1,0:T(8,128)(2,1)}, bf16[16,4096]{1,0:T(8,128)(2,1)}, bf16[16,4096]{1,0:T(8,128)(2,1)}, bf16[16,4096]{1,0:T(8,128)(2,1)}) custom-call(bf16[64,1024]{1,0:T(8,128)(2,1)} %subtract_convert_fusion.diff, bf16[8192,1024]{1,0:T(8,128)(2,1)} %refs_3_.5, bf16[8192,1024]{1,0:T(8,128)(2,1)} %refs_3_.5, bf16[8192,1024]{1,0:T(8,128)(2,1)} %refs_3_.5, ...), custom_call_target="tpu_custom_call" | custom-call | flops 536870912 | bytes 8912896 | tf_op jit(solution)/shard_map/pallas_call | solution.py:414
  230.2 1.5 collective-permute-start.43
  231.6 1.2 collective-permute-start.44
  233.0 1.0 collective-permute-start.45
  234.0 2.4 collective-permute-start.46
  236.4 2.3 collective-permute-start.47
  238.7 1.0 convert_add_fusion.1
  (176 shorter events, 22.6 us)
Async XLA Ops:
  0.6 26.8 %collective-permute-start = (bf16[64,8192]{1,0:T(8,128)(2,1)}, bf16[64,8192]{1,0:T(8,128)(2,1)}, u32[]{:S(2)}, u32[]{:S(2)}) collective-permute-start(bf16[64,8192]{1,0:T(8,128)(2,1)} %refs_0_.3), channel_id=1, source_target_pairs={{0,2},{1,3},{2,0},{3,1},{4,5},{5,4},{6,7},{7,6},{8,10},{9,11},{10,... | collective-permute-start | bytes 3145736 | tf_op jit(solution)/shard_map/ppermute | solution.py:285
  3.7 23.8 %collective-permute-start.1 = (bf16[64,8192]{1,0:T(8,128)(2,1)}, bf16[64,8192]{1,0:T(8,128)(2,1)}, u32[]{:S(2)}, u32[]{:S(2)}) collective-permute-start(bf16[64,8192]{1,0:T(8,128)(2,1)} %refs_0_.3), channel_id=1, source_target_pairs={{0,1},{1,0},{2,3},{3,2},{4,6},{5,7},{6,4},{7,5},{8,9},{9,8},{10,11... | collective-permute-start | bytes 3145736 | tf_op jit(solution)/shard_map/ppermute | solution.py:288
  5.2 26.4 %collective-permute-start.2 = (bf16[64,8192]{1,0:T(8,128)(2,1)}, bf16[64,8192]{1,0:T(8,128)(2,1)S(1)}, u32[]{:S(2)}, u32[]{:S(2)}) collective-permute-start(bf16[64,8192]{1,0:T(8,128)(2,1)} %refs_0_.3), channel_id=1, source_target_pairs={{0,8},{8,16},{16,24},{24,0},{1,9},{9,17},{17,25},{25,1},{2,10},{10... | collective-permute-start | bytes 3145736 | tf_op jit(solution)/shard_map/ppermute | solution.py:24
  6.7 29.6 %collective-permute-start.7 = (bf16[64,8192]{1,0:T(8,128)(2,1)}, bf16[64,8192]{1,0:T(8,128)(2,1)}, u32[]{:S(2)}, u32[]{:S(2)}) collective-permute-start(bf16[64,8192]{1,0:T(8,128)(2,1)} %refs_0_.3), channel_id=1, source_target_pairs={{0,4},{4,0},{1,5},{5,1},{2,6},{6,2},{3,7},{7,3},{8,12},{12,8},{9,1... | collective-permute-start | bytes 3145736 | tf_op jit(solution)/shard_map/ppermute | solution.py:19
  31.6 6.2 %collective-permute-start.8 = (bf16[64,8192]{1,0:T(8,128)(2,1)}, bf16[64,8192]{1,0:T(8,128)(2,1)}, u32[]{:S(2)}, u32[]{:S(2)}) collective-permute-start(bf16[64,8192]{1,0:T(8,128)(2,1)} %collective-permute-done.refs_2_), channel_id=1, source_target_pairs={{0,4},{4,0},{1,5},{5,1},{2,6},{6,2},{3,7},{7,3},{8,12},{12,8},{9,1... | collective-permute-start | bytes 3145736 | tf_op jit(solution)/shard_map/ppermute | solution.py:19
  31.6 6.2 %collective-permute-start.9 = (bf16[64,8192]{1,0:T(8,128)(2,1)}, bf16[64,8192]{1,0:T(8,128)(2,1)}, u32[]{:S(2)}, u32[]{:S(2)}) collective-permute-start(bf16[64,8192]{1,0:T(8,128)(2,1)} %collective-permute-done.1.refs_4_), channel_id=1, source_target_pairs={{0,4},{4,0},{1,5},{5,1},{2,6},{6,2},{3,7},{7,3},{8,12},{12,8},{9,1... | collective-permute-start | bytes 3145736 | tf_op jit(solution)/shard_map/ppermute | solution.py:19
  33.6 29.9 %collective-permute-start.3 = (bf16[64,8192]{1,0:T(8,128)(2,1)S(1)}, bf16[64,8192]{1,0:T(8,128)(2,1)}, u32[]{:S(2)}, u32[]{:S(2)}) collective-permute-start(bf16[64,8192]{1,0:T(8,128)(2,1)S(1)} %collective-permute-done.2.refs_2_), channel_id=1, source_target_pairs={{0,2},{1,3},{2,0},{3,1},{4,5},{5,4},{6,7},{7,6},{8,10},{9,11},{10,... | collective-permute-start | bytes 3145736 | tf_op jit(solution)/shard_map/ppermute | solution.py:285
  34.2 29.3 %collective-permute-start.4 = (bf16[64,8192]{1,0:T(8,128)(2,1)S(1)}, bf16[64,8192]{1,0:T(8,128)(2,1)}, u32[]{:S(2)}, u32[]{:S(2)}) collective-permute-start(bf16[64,8192]{1,0:T(8,128)(2,1)S(1)} %collective-permute-done.2.refs_2_), channel_id=1, source_target_pairs={{0,1},{1,0},{2,3},{3,2},{4,6},{5,7},{6,4},{7,5},{8,9},{9,8},{10,11... | collective-permute-start | bytes 3145736 | tf_op jit(solution)/shard_map/ppermute | solution.py:288
  36.4 33.8 %collective-permute-start.5 = (bf16[64,8192]{1,0:T(8,128)(2,1)}, bf16[64,8192]{1,0:T(8,128)(2,1)}, u32[]{:S(2)}, u32[]{:S(2)}) collective-permute-start(bf16[64,8192]{1,0:T(8,128)(2,1)} %collective-permute-done.refs_2_), channel_id=1, source_target_pairs={{0,1},{1,0},{2,3},{3,2},{4,6},{5,7},{6,4},{7,5},{8,9},{9,8},{10,11... | collective-permute-start | bytes 3145736 | tf_op jit(solution)/shard_map/ppermute | solution.py:288
  37.9 36.6 %collective-permute-start.15 = (bf16[64,8192]{1,0:T(8,128)(2,1)S(1)}, bf16[64,8192]{1,0:T(8,128)(2,1)}, u32[]{:S(2)}, u32[]{:S(2)}) collective-permute-start(bf16[64,8192]{1,0:T(8,128)(2,1)S(1)} %collective-permute-done.2.refs_2_), channel_id=1, source_target_pairs={{0,4},{4,0},{1,5},{5,1},{2,6},{6,2},{3,7},{7,3},{8,12},{12,8},{9,1... | collective-permute-start | bytes 3145736 | tf_op jit(solution)/shard_map/ppermute | solution.py:19
  37.9 25.7 %collective-permute-start.6 = (bf16[64,8192]{1,0:T(8,128)(2,1)S(1)}, bf16[64,8192]{1,0:T(8,128)(2,1)}, u32[]{:S(2)}, u32[]{:S(2)}) collective-permute-start(bf16[64,8192]{1,0:T(8,128)(2,1)S(1)} %copy-done.13), channel_id=1, source_target_pairs={{0,24},{8,0},{16,8},{24,16},{1,25},{9,1},{17,9},{25,17},{2,26},{10... | collective-permute-start | bytes 3145736 | tf_op jit(solution)/shard_map/ppermute | solution.py:24
  70.1 3.7 %collective-permute-start.14 = (bf16[64,8192]{1,0:T(8,128)(2,1)}, bf16[64,8192]{1,0:T(8,128)(2,1)S(1)}, u32[]{:S(2)}, u32[]{:S(2)}) collective-permute-start(bf16[64,8192]{1,0:T(8,128)(2,1)} %collective-permute-done.5.refs_0_), channel_id=1, source_target_pairs={{0,4},{4,0},{1,5},{5,1},{2,6},{6,2},{3,7},{7,3},{8,12},{12,8},{9,1... | collective-permute-start | bytes 3145736 | tf_op jit(solution)/shard_map/ppermute | solution.py:19
  70.2 5.7 %collective-permute-start.16 = (bf16[64,8192]{1,0:T(8,128)(2,1)}, bf16[64,8192]{1,0:T(8,128)(2,1)}, u32[]{:S(2)}, u32[]{:S(2)}) collective-permute-start(bf16[64,8192]{1,0:T(8,128)(2,1)} %collective-permute-done.3.refs_4_), channel_id=1, source_target_pairs={{0,4},{4,0},{1,5},{5,1},{2,6},{6,2},{3,7},{7,3},{8,12},{12,8},{9,1... | collective-permute-start | bytes 3145736 | tf_op jit(solution)/shard_map/ppermute | solution.py:19
  70.6 5.5 %collective-permute-start.17 = (bf16[64,8192]{1,0:T(8,128)(2,1)}, bf16[64,8192]{1,0:T(8,128)(2,1)}, u32[]{:S(2)}, u32[]{:S(2)}) collective-permute-start(bf16[64,8192]{1,0:T(8,128)(2,1)} %collective-permute-done.4.refs_6_), channel_id=1, source_target_pairs={{0,4},{4,0},{1,5},{5,1},{2,6},{6,2},{3,7},{7,3},{8,12},{12,8},{9,1... | collective-permute-start | bytes 3145736 | tf_op jit(solution)/shard_map/ppermute | solution.py:19
  70.9 30.4 %collective-permute-start.12 = (bf16[64,8192]{1,0:T(8,128)(2,1)}, bf16[64,8192]{1,0:T(8,128)(2,1)}, u32[]{:S(2)}, u32[]{:S(2)}) collective-permute-start(bf16[64,8192]{1,0:T(8,128)(2,1)} %collective-permute-done.3.refs_4_), channel_id=1, source_target_pairs={{0,1},{1,0},{2,3},{3,2},{4,6},{5,7},{6,4},{7,5},{8,9},{9,8},{10,11... | collective-permute-start | bytes 3145736 | tf_op jit(solution)/shard_map/ppermute | solution.py:288
  73.8 27.4 %collective-permute-start.10 = (bf16[64,8192]{1,0:T(8,128)(2,1)}, bf16[64,8192]{1,0:T(8,128)(2,1)}, u32[]{:S(2)}, u32[]{:S(2)}) collective-permute-start(bf16[64,8192]{1,0:T(8,128)(2,1)} %collective-permute-done.6.refs_2_), channel_id=1, source_target_pairs={{0,2},{1,3},{2,0},{3,1},{4,5},{5,4},{6,7},{7,6},{8,10},{9,11},{10,... | collective-permute-start | bytes 3145736 | tf_op jit(solution)/shard_map/ppermute | solution.py:285
  74.4 34.1 %collective-permute-start.11 = (bf16[64,8192]{1,0:T(8,128)(2,1)}, bf16[64,8192]{1,0:T(8,128)(2,1)}, u32[]{:S(2)}, u32[]{:S(2)}) collective-permute-start(bf16[64,8192]{1,0:T(8,128)(2,1)} %collective-permute-done.6.refs_2_), channel_id=1, source_target_pairs={{0,1},{1,0},{2,3},{3,2},{4,6},{5,7},{6,4},{7,5},{8,9},{9,8},{10,11... | collective-permute-start | bytes 3145736 | tf_op jit(solution)/shard_map/ppermute | solution.py:288
  75.9 33.8 %collective-permute-start.23 = (bf16[64,8192]{1,0:T(8,128)(2,1)}, bf16[64,8192]{1,0:T(8,128)(2,1)}, u32[]{:S(2)}, u32[]{:S(2)}) collective-permute-start(bf16[64,8192]{1,0:T(8,128)(2,1)} %collective-permute-done.6.refs_2_), channel_id=1, source_target_pairs={{0,4},{4,0},{1,5},{5,1},{2,6},{6,2},{3,7},{7,3},{8,12},{12,8},{9,1... | collective-permute-start | bytes 3145736 | tf_op jit(solution)/shard_map/ppermute | solution.py:19
  76.1 32.4 %collective-permute-start.13 = (bf16[64,8192]{1,0:T(8,128)(2,1)S(1)}, bf16[64,8192]{1,0:T(8,128)(2,1)S(1)}, u32[]{:S(2)}, u32[]{:S(2)}) collective-permute-start(bf16[64,8192]{1,0:T(8,128)(2,1)S(1)} %collective-permute-done.2.refs_2_), channel_id=1, source_target_pairs={{0,8},{8,16},{16,24},{24,0},{1,9},{9,17},{17,25},{25,1},{2,10},{10... | collective-permute-start | bytes 3145736 | tf_op jit(solution)/shard_map/ppermute | solution.py:24
  108.5 2.9 %collective-permute-start.22 = (bf16[64,8192]{1,0:T(8,128)(2,1)}, bf16[64,8192]{1,0:T(8,128)(2,1)S(1)}, u32[]{:S(2)}, u32[]{:S(2)}) collective-permute-start(bf16[64,8192]{1,0:T(8,128)(2,1)} %collective-permute-done.12.refs_0_), channel_id=1, source_target_pairs={{0,4},{4,0},{1,5},{5,1},{2,6},{6,2},{3,7},{7,3},{8,12},{12,8},{9,1... | collective-permute-start | bytes 3145736 | tf_op jit(solution)/shard_map/ppermute | solution.py:19
  108.6 4.4 %collective-permute-start.24 = (bf16[64,8192]{1,0:T(8,128)(2,1)}, bf16[64,8192]{1,0:T(8,128)(2,1)S(1)}, u32[]{:S(2)}, u32[]{:S(2)}) collective-permute-start(bf16[64,8192]{1,0:T(8,128)(2,1)} %collective-permute-done.10.refs_4_), channel_id=1, source_target_pairs={{0,4},{4,0},{1,5},{5,1},{2,6},{6,2},{3,7},{7,3},{8,12},{12,8},{9,1... | collective-permute-start | bytes 3145736 | tf_op jit(solution)/shard_map/ppermute | solution.py:19
  109.1 5.4 %collective-permute-start.25 = (bf16[64,8192]{1,0:T(8,128)(2,1)}, bf16[64,8192]{1,0:T(8,128)(2,1)S(1)}, u32[]{:S(2)}, u32[]{:S(2)}) collective-permute-start(bf16[64,8192]{1,0:T(8,128)(2,1)} %collective-permute-done.11.refs_6_), channel_id=1, source_target_pairs={{0,4},{4,0},{1,5},{5,1},{2,6},{6,2},{3,7},{7,3},{8,12},{12,8},{9,1... | collective-permute-start | bytes 3145736 | tf_op jit(solution)/shard_map/ppermute | solution.py:19
  109.2 31.5 %collective-permute-start.18 = (bf16[64,8192]{1,0:T(8,128)(2,1)S(1)}, bf16[64,8192]{1,0:T(8,128)(2,1)S(1)}, u32[]{:S(2)}, u32[]{:S(2)}) collective-permute-start(bf16[64,8192]{1,0:T(8,128)(2,1)S(1)} %collective-permute-done.13.refs_2_), channel_id=1, source_target_pairs={{0,2},{1,3},{2,0},{3,1},{4,5},{5,4},{6,7},{7,6},{8,10},{9,11},{10,... | collective-permute-start | bytes 3145736 | tf_op jit(solution)/shard_map/ppermute | solution.py:285
  109.7 31.0 %collective-permute-start.19 = (bf16[64,8192]{1,0:T(8,128)(2,1)S(1)}, bf16[64,8192]{1,0:T(8,128)(2,1)S(1)}, u32[]{:S(2)}, u32[]{:S(2)}) collective-permute-start(bf16[64,8192]{1,0:T(8,128)(2,1)S(1)} %collective-permute-done.13.refs_2_), channel_id=1, source_target_pairs={{0,1},{1,0},{2,3},{3,2},{4,6},{5,7},{6,4},{7,5},{8,9},{9,8},{10,11... | collective-permute-start | bytes 3145736 | tf_op jit(solution)/shard_map/ppermute | solution.py:288
  111.5 29.3 %collective-permute-start.20 = (bf16[64,8192]{1,0:T(8,128)(2,1)}, bf16[64,8192]{1,0:T(8,128)(2,1)}, u32[]{:S(2)}, u32[]{:S(2)}) collective-permute-start(bf16[64,8192]{1,0:T(8,128)(2,1)} %collective-permute-done.12.refs_0_), channel_id=1, source_target_pairs={{0,8},{8,16},{16,24},{24,0},{1,9},{9,17},{17,25},{25,1},{2,10},{10... | collective-permute-start | bytes 3145736 | tf_op jit(solution)/shard_map/ppermute | solution.py:24
  113.0 33.1 %collective-permute-start.21 = (bf16[64,8192]{1,0:T(8,128)(2,1)}, bf16[64,8192]{1,0:T(8,128)(2,1)}, u32[]{:S(2)}, u32[]{:S(2)}) collective-permute-start(bf16[64,8192]{1,0:T(8,128)(2,1)} %collective-permute-done.10.refs_4_), channel_id=1, source_target_pairs={{0,1},{1,0},{2,3},{3,2},{4,6},{5,7},{6,4},{7,5},{8,9},{9,8},{10,11... | collective-permute-start | bytes 3145736 | tf_op jit(solution)/shard_map/ppermute | solution.py:288
  115.4 31.9 %collective-permute-start.27 = (bf16[64,8192]{1,0:T(8,128)(2,1)S(1)}, bf16[64,8192]{1,0:T(8,128)(2,1)}, u32[]{:S(2)}, u32[]{:S(2)}) collective-permute-start(bf16[64,8192]{1,0:T(8,128)(2,1)S(1)} %collective-permute-done.13.refs_2_), channel_id=1, source_target_pairs={{0,4},{4,0},{1,5},{5,1},{2,6},{6,2},{3,7},{7,3},{8,12},{12,8},{9,1... | collective-permute-start | bytes 3145736 | tf_op jit(solution)/shard_map/ppermute | solution.py:19
  146.0 3.0 %collective-permute-start.26 = (bf16[64,8192]{1,0:T(8,128)(2,1)}, bf16[64,8192]{1,0:T(8,128)(2,1)}, u32[]{:S(2)}, u32[]{:S(2)}) collective-permute-start(bf16[64,8192]{1,0:T(8,128)(2,1)} %collective-permute-done.21.refs_0_), channel_id=1, source_target_pairs={{0,4},{4,0},{1,5},{5,1},{2,6},{6,2},{3,7},{7,3},{8,12},{12,8},{9,1... | collective-permute-start | bytes 3145736 | tf_op jit(solution)/shard_map/ppermute | solution.py:19
  146.4 5.4 %collective-permute-start.28 = (bf16[64,8192]{1,0:T(8,128)(2,1)S(1)}, bf16[64,8192]{1,0:T(8,128)(2,1)}, u32[]{:S(2)}, u32[]{:S(2)}) collective-permute-start(bf16[64,8192]{1,0:T(8,128)(2,1)S(1)} %collective-permute-done.18.refs_4_), channel_id=1, source_target_pairs={{0,4},{4,0},{1,5},{5,1},{2,6},{6,2},{3,7},{7,3},{8,12},{12,8},{9,1... | collective-permute-start | bytes 3145736 | tf_op jit(solution)/shard_map/ppermute | solution.py:19
  146.5 6.8 %collective-permute-start.29 = (bf16[64,8192]{1,0:T(8,128)(2,1)S(1)}, bf16[64,8192]{1,0:T(8,128)(2,1)}, u32[]{:S(2)}, u32[]{:S(2)}) collective-permute-start(bf16[64,8192]{1,0:T(8,128)(2,1)S(1)} %collective-permute-done.19.refs_6_), channel_id=1, source_target_pairs={{0,4},{4,0},{1,5},{5,1},{2,6},{6,2},{3,7},{7,3},{8,12},{12,8},{9,1... | collective-permute-start | bytes 3145736 | tf_op jit(solution)/shard_map/ppermute | solution.py:19
  146.9 6.4 %collective-permute-start.30 = (bf16[64,8192]{1,0:T(8,128)(2,1)}, bf16[64,8192]{1,0:T(8,128)(2,1)}, u32[]{:S(2)}, u32[]{:S(2)}) collective-permute-start(bf16[64,8192]{1,0:T(8,128)(2,1)} %collective-permute-done.20.refs_8_), channel_id=1, source_target_pairs={{0,4},{4,0},{1,5},{5,1},{2,6},{6,2},{3,7},{7,3},{8,12},{12,8},{9,1... | collective-permute-start | bytes 3145736 | tf_op jit(solution)/shard_map/ppermute | solution.py:19
  189.2 2.0 collective-permute-start.31
  191.4 4.6 %collective-permute-start.32 = (bf16[32,1152]{1,0:T(8,128)(2,1)S(1)}, bf16[32,1152]{1,0:T(8,128)(2,1)S(1)}, u32[]{:S(2)}, u32[]{:S(2)}) collective-permute-start(bf16[32,1152]{1,0:T(8,128)(2,1)S(1)} %concatenate.83), channel_id=1, source_target_pairs={{0,1},{1,0},{2,3},{3,2},{4,5},{5,4},{6,7},{7,6},{8,9},{9,8},{10,11... | collective-permute-start | bytes 221192 | tf_op jit(solution)/shard_map/ppermute | solution.py:19
  192.8 5.4 %collective-permute-start.33 = (bf16[32,1152]{1,0:T(8,128)(2,1)S(1)}, bf16[32,1152]{1,0:T(8,128)(2,1)S(1)}, u32[]{:S(2)}, u32[]{:S(2)}) collective-permute-start(bf16[32,1152]{1,0:T(8,128)(2,1)S(1)} %concatenate.84), channel_id=1, source_target_pairs={{0,2},{1,3},{2,0},{3,1},{4,6},{5,7},{6,4},{7,5},{8,10},{9,11},{10,... | collective-permute-start | bytes 221192 | tf_op jit(solution)/shard_map/ppermute | solution.py:19
  193.5 5.3 %collective-permute-start.34 = (bf16[32,1152]{1,0:T(8,128)(2,1)S(1)}, bf16[32,1152]{1,0:T(8,128)(2,1)S(1)}, u32[]{:S(2)}, u32[]{:S(2)}) collective-permute-start(bf16[32,1152]{1,0:T(8,128)(2,1)S(1)} %concatenate.85), channel_id=1, source_target_pairs={{0,3},{1,2},{2,1},{3,0},{4,7},{5,6},{6,5},{7,4},{8,11},{9,10},{10,... | collective-permute-start | bytes 221192 | tf_op jit(solution)/shard_map/ppermute | solution.py:19
  199.1 7.9 %collective-permute-start.36 = (bf16[4,8,1152]{2,1,0:T(8,128)(2,1)S(1)}, bf16[4,8,1152]{2,1,0:T(8,128)(2,1)S(1)}, u32[]{:S(2)}, u32[]{:S(2)}) collective-permute-start(bf16[4,8,1152]{2,1,0:T(8,128)(2,1)S(1)} %concatenate.86), channel_id=1, source_target_pairs={{0,16},{8,24},{16,0},{24,8},{1,17},{9,25},{17,1},{25,9},{2,18},{10... | collective-permute-start | bytes 221192 | tf_op jit(solution)/shard_map/ppermute | solution.py:24
  199.8 6.3 %collective-permute-start.35 = (bf16[4,8,1152]{2,1,0:T(8,128)(2,1)S(1)}, bf16[4,8,1152]{2,1,0:T(8,128)(2,1)S(1)}, u32[]{:S(2)}, u32[]{:S(2)}) collective-permute-start(bf16[4,8,1152]{2,1,0:T(8,128)(2,1)S(1)} %concatenate.86), channel_id=1, source_target_pairs={{0,8},{8,16},{16,24},{24,0},{1,9},{9,17},{17,25},{25,1},{2,10},{10... | collective-permute-start | bytes 221192 | tf_op jit(solution)/shard_map/ppermute | solution.py:24
  201.3 5.6 %collective-permute-start.37 = (bf16[4,8,1152]{2,1,0:T(8,128)(2,1)S(1)}, bf16[4,8,1152]{2,1,0:T(8,128)(2,1)S(1)}, u32[]{:S(2)}, u32[]{:S(2)}) collective-permute-start(bf16[4,8,1152]{2,1,0:T(8,128)(2,1)S(1)} %concatenate.86), channel_id=1, source_target_pairs={{0,24},{8,0},{16,8},{24,16},{1,25},{9,1},{17,9},{25,17},{2,26},{10... | collective-permute-start | bytes 221192 | tf_op jit(solution)/shard_map/ppermute | solution.py:24
  207.2 1.4 collective-permute-start.38
  219.3 12.4 %collective-permute-start.39 = (bf16[16,5120]{1,0:T(8,128)(2,1)}, bf16[16,5120]{1,0:T(8,128)(2,1)S(1)}, u32[]{:S(2)}, u32[]{:S(2)}) collective-permute-start(bf16[16,5120]{1,0:T(8,128)(2,1)} %get-tuple-element.101), channel_id=1, source_target_pairs={{0,1},{1,0},{2,3},{3,2},{4,5},{5,4},{6,7},{7,6},{8,9},{9,8},{10,11... | collective-permute-start | bytes 491528 | tf_op jit(solution)/shard_map/ppermute | solution.py:19
  220.1 12.8 %collective-permute-start.40 = (bf16[16,5120]{1,0:T(8,128)(2,1)}, bf16[16,5120]{1,0:T(8,128)(2,1)S(1)}, u32[]{:S(2)}, u32[]{:S(2)}) collective-permute-start(bf16[16,5120]{1,0:T(8,128)(2,1)} %get-tuple-element.102), channel_id=1, source_target_pairs={{0,2},{1,3},{2,0},{3,1},{4,6},{5,7},{6,4},{7,5},{8,10},{9,11},{10,... | collective-permute-start | bytes 491528 | tf_op jit(solution)/shard_map/ppermute | solution.py:19
  221.6 11.3 %collective-permute-start.41 = (bf16[16,5120]{1,0:T(8,128)(2,1)}, bf16[16,5120]{1,0:T(8,128)(2,1)S(1)}, u32[]{:S(2)}, u32[]{:S(2)}) collective-permute-start(bf16[16,5120]{1,0:T(8,128)(2,1)} %get-tuple-element.103), channel_id=1, source_target_pairs={{0,3},{1,2},{2,1},{3,0},{4,7},{5,6},{6,5},{7,4},{8,11},{9,10},{10,... | collective-permute-start | bytes 491528 | tf_op jit(solution)/shard_map/ppermute | solution.py:19
  229.3 7.1 %collective-permute-start.42 = (bf16[16,4096]{1,0:T(8,128)(2,1)}, bf16[16,4096]{1,0:T(8,128)(2,1)S(1)}, u32[]{:S(2)}, u32[]{:S(2)}) collective-permute-start(bf16[16,4096]{1,0:T(8,128)(2,1)} %get-tuple-element.105), channel_id=1, source_target_pairs={{0,1},{1,0},{2,3},{3,2},{4,5},{5,4},{6,7},{7,6},{8,9},{9,8},{10,11... | collective-permute-start | bytes 393224 | tf_op jit(solution)/shard_map/ppermute | solution.py:19
  230.2 8.5 %collective-permute-start.43 = (bf16[16,4096]{1,0:T(8,128)(2,1)}, bf16[16,4096]{1,0:T(8,128)(2,1)S(1)}, u32[]{:S(2)}, u32[]{:S(2)}) collective-permute-start(bf16[16,4096]{1,0:T(8,128)(2,1)} %get-tuple-element.106), channel_id=1, source_target_pairs={{0,2},{1,3},{2,0},{3,1},{4,6},{5,7},{6,4},{7,5},{8,10},{9,11},{10,... | collective-permute-start | bytes 393224 | tf_op jit(solution)/shard_map/ppermute | solution.py:19
  231.6 7.1 %collective-permute-start.44 = (bf16[16,4096]{1,0:T(8,128)(2,1)}, bf16[16,4096]{1,0:T(8,128)(2,1)S(1)}, u32[]{:S(2)}, u32[]{:S(2)}) collective-permute-start(bf16[16,4096]{1,0:T(8,128)(2,1)} %get-tuple-element.107), channel_id=1, source_target_pairs={{0,3},{1,2},{2,1},{3,0},{4,7},{5,6},{6,5},{7,4},{8,11},{9,10},{10,... | collective-permute-start | bytes 393224 | tf_op jit(solution)/shard_map/ppermute | solution.py:19
  233.0 6.7 %collective-permute-start.45 = (f32[16,512]{1,0:T(8,128)S(1)}, f32[16,512]{1,0:T(8,128)S(1)}, u32[]{:S(2)}, u32[]{:S(2)}) collective-permute-start(f32[16,512]{1,0:T(8,128)S(1)} %slice_add_fusion.1), channel_id=1, source_target_pairs={{0,8},{8,16},{16,24},{24,0},{1,9},{9,17},{17,25},{25,1},{2,10},{10... | collective-permute-start | bytes 98312 | tf_op jit(solution)/shard_map/ppermute | solution.py:24
  234.0 5.7 %collective-permute-start.46 = (f32[16,512]{1,0:T(8,128)S(1)}, f32[16,512]{1,0:T(8,128)S(1)}, u32[]{:S(2)}, u32[]{:S(2)}) collective-permute-start(f32[16,512]{1,0:T(8,128)S(1)} %slice_add_fusion.1), channel_id=1, source_target_pairs={{0,16},{8,24},{16,0},{24,8},{1,17},{9,25},{17,1},{25,9},{2,18},{10... | collective-permute-start | bytes 98312 | tf_op jit(solution)/shard_map/ppermute | solution.py:24
  236.4 3.9 %collective-permute-start.47 = (f32[16,512]{1,0:T(8,128)S(1)}, f32[16,512]{1,0:T(8,128)S(1)}, u32[]{:S(2)}, u32[]{:S(2)}) collective-permute-start(f32[16,512]{1,0:T(8,128)S(1)} %slice_add_fusion.1), channel_id=1, source_target_pairs={{0,24},{8,0},{16,8},{24,16},{1,25},{9,1},{17,9},{25,17},{2,26},{10... | collective-permute-start | bytes 98312 | tf_op jit(solution)/shard_map/ppermute | solution.py:24
  (23 other events, 402.1 us)
